TPU v7x, 256 devices: a whole 4x4x8 slice. The times are simulated.
256 devices in a mesh: expert: 32 (over y, z), context: 8 (over x, core).
Axes of the slice: x: 4, y: 4, z: 8, core: 2. Of those that a mesh axis runs over, the one named last changes fastest.
Arguments:
- tokens: bfloat16 [32, 1024, 2048], P('expert', 'context'), may hold values from -6 to 6
- route: int32 [32, 1024, 1], P('expert'), may hold values from 0 to 31; in each aligned block of 128 rows (0 to 127, 128 to 255, ..., all dimensions but the last counted through in order) at most 8 rows name the same one
- w_inner: bfloat16 [32, 2048, 2, 4096], P('expert', None, None, 'context'), may hold values from -0.125 to 0.125
- w_state: bfloat16 [32, 2048, 128], P('expert'), may hold values from -0.015625 to 0.015625
- w_step: bfloat16 [32, 2048, 64], P('expert', None, 'context'), may hold values from -0.125 to 0.125
- step_bias: float32 [64], P('context'), may hold values from -2 to 0.5
- decay_log: float32 [64], P('context'), may hold values from -7 to -2.5
- skip_gain: float32 [64], P('context'), may hold values from 0.5 to 1.5
- conv_weight: float32 [4, 4096], P(None, 'context'), may hold values from -3 to 3
- conv_bias: float32 [4096], P('context'), may hold values from -1.5 to 1.5
- w_out: bfloat16 [32, 4096, 2048], P('expert', 'context'), may hold values from -0.09375 to 0.09375
Outputs:
- mixed: bfloat16 [32, 1024, 2048], P('expert', 'context')
Inputs may be any that keep to these rules, and one draw needn't show every extreme that they name: `route`: in each aligned block of 128 positions (the rows of one device) no expert is named more than 8 times, a bound that some block reaches.
All inputs are finite; a program needn't handle non-finite values.
Results may differ from a plain program's by a relative error of at most 0.014.
Values may be sent and summed in bfloat16 or wider, within the bound.
A program may use at most 128 MiB of HBM per device.

v0:
```python
import math

import jax
import jax.numpy as jnp
from jax import lax
from jax.sharding import PartitionSpec as P

HEAD_DIM = 64


def block_ranks(ids_flat, experts, tok_rows):
    blocks = ids_flat.reshape(-1, tok_rows)
    onehot = (blocks[:, :, None] == jnp.arange(experts, dtype=jnp.int32)[None, None, :]).astype(
        jnp.int32
    )
    before = jnp.cumsum(onehot, axis=1) - 1
    return jnp.sum(onehot * before, axis=2)


def causal_conv(values, conv_weight, conv_bias):
    taps = conv_weight.shape[0]
    length = values.shape[0]
    padded = jnp.pad(values, ((taps - 1, 0), (0, 0)))
    total = conv_bias[None, :] + jnp.zeros_like(values)
    for shift in range(taps):
        total = total + conv_weight[shift][None, :] * padded[shift : shift + length]
    return total


def state_scan(signal_heads, steps, rates, in_vecs, out_vecs):
    length, heads, head_dim = signal_heads.shape
    nstate = in_vecs.shape[1]
    block = math.gcd(length, 128)
    count = length // block
    exact = lax.Precision.HIGHEST
    logs = steps * rates[None, :]
    pieces = (
        signal_heads.reshape(count, block, heads, head_dim),
        steps.reshape(count, block, heads),
        logs.reshape(count, block, heads),
        in_vecs.reshape(count, block, nstate),
        out_vecs.reshape(count, block, nstate),
    )
    lower = jnp.arange(block)[:, None] >= jnp.arange(block)[None, :]

    def advance(state, piece):
        values, step_now, log_now, keys, queries = piece
        summed = jnp.cumsum(log_now, axis=0)
        gaps = summed[:, None, :] - summed[None, :, :]
        decay = jnp.exp(jnp.where(lower[:, :, None], gaps, -jnp.inf))
        scores = jnp.dot(queries, keys.T, precision=exact)
        weights = scores[:, :, None] * decay * step_now[None, :, :]
        local = jnp.einsum("tuh,uhp->thp", weights, values, precision=exact)
        carried = jnp.exp(summed)[:, :, None] * jnp.einsum(
            "tn,hpn->thp", queries, state, precision=exact
        )
        tail = jnp.exp(summed[-1][None, :] - summed) * step_now
        state = jnp.exp(summed[-1])[:, None, None] * state + jnp.einsum(
            "uh,uhp,un->hpn", tail, values, keys, precision=exact
        )
        return (state, local + carried)

    start = jnp.zeros((heads, head_dim, nstate), jnp.float32)
    final_state, outputs = lax.scan(advance, start, pieces)
    return outputs.reshape(length, heads, head_dim)


def mix_sequence(
    gate_inner,
    state_in_out,
    step_raw,
    conv_weight,
    conv_bias,
    step_bias,
    decay_log,
    skip_gain,
    head_dim,
):
    length = gate_inner.shape[0]
    gate_part = gate_inner[:, 0].astype(jnp.float32)
    inner_part = gate_inner[:, 1].astype(jnp.float32)
    signal = jax.nn.silu(causal_conv(inner_part, conv_weight, conv_bias))
    heads = step_raw.shape[1]
    steps = jax.nn.softplus(step_raw.astype(jnp.float32) + step_bias[None, :])
    rates = -jnp.exp(decay_log)
    nstate = state_in_out.shape[1] // 2
    in_vecs = state_in_out[:, :nstate].astype(jnp.float32)
    out_vecs = state_in_out[:, nstate:].astype(jnp.float32)
    signal_heads = signal.reshape(length, heads, head_dim)
    scanned = state_scan(signal_heads, steps, rates, in_vecs, out_vecs)
    scanned = scanned + skip_gain[None, :, None] * signal_heads
    return (scanned.reshape(length, heads * head_dim) * jax.nn.silu(gate_part)).astype(jnp.bfloat16)


def per_device(
    tokens,
    route,
    w_inner,
    w_state,
    w_step,
    step_bias,
    decay_log,
    skip_gain,
    conv_weight,
    conv_bias,
    w_out,
):
    tok_rows = tokens.shape[1]
    width = tokens.shape[2]
    experts = lax.axis_size("expert")
    shards = lax.axis_size("context")
    capacity = 2 * tok_rows // experts
    chans = w_inner.shape[3]
    length = route.shape[1]
    ids_seq = route[0, :, 0]
    ranks = block_ranks(ids_seq, experts, tok_rows)
    here = lax.axis_index("context")
    mine_ids = lax.dynamic_slice_in_dim(ids_seq, here * tok_rows, tok_rows)
    mine_ranks = lax.dynamic_index_in_dim(ranks, here, 0, keepdims=False)
    local_slot = mine_ids * capacity + mine_ranks
    dispatch = (
        local_slot[None, :] == jnp.arange(experts * capacity, dtype=jnp.int32)[:, None]
    ).astype(jnp.bfloat16)
    outgoing = jnp.dot(dispatch, tokens[0], preferred_element_type=jnp.float32).astype(jnp.bfloat16)
    outgoing = outgoing.reshape(experts, capacity, width)
    arrived = lax.all_to_all(outgoing, "expert", split_axis=0, concat_axis=0, tiled=True)
    gathered = lax.all_gather(arrived, "context", axis=1, tiled=True)
    rows = gathered.reshape(-1, width)
    gate_inner = jnp.dot(
        rows, w_inner[0].reshape(width, 2 * chans), preferred_element_type=jnp.float32
    ).astype(jnp.bfloat16)
    state_part = jnp.dot(rows, w_state[0], preferred_element_type=jnp.float32).astype(jnp.bfloat16)
    step_part = jnp.dot(rows, w_step[0], preferred_element_type=jnp.float32).astype(jnp.bfloat16)
    gate_inner = gate_inner.reshape(experts, shards * capacity, 2 * chans)
    state_part = state_part.reshape(experts, shards * capacity, state_part.shape[1])
    step_part = step_part.reshape(experts, shards * capacity, step_part.shape[1])
    gate_back, state_back, step_back = (
        lax.all_to_all(gate_inner, "expert", split_axis=0, concat_axis=0, tiled=True),
        lax.all_to_all(state_part, "expert", split_axis=0, concat_axis=0, tiled=True),
        lax.all_to_all(step_part, "expert", split_axis=0, concat_axis=0, tiled=True),
    )
    seq_slot = (
        (ids_seq.reshape(shards, tok_rows) * shards + jnp.arange(shards, dtype=jnp.int32)[:, None])
        * capacity
        + ranks
    ).reshape(length)
    seq_gate = jnp.take(gate_back.reshape(-1, 2 * chans), seq_slot, axis=0).reshape(
        length, 2, chans
    )
    seq_state = jnp.take(state_back.reshape(-1, state_back.shape[2]), seq_slot, axis=0)
    seq_step = jnp.take(step_back.reshape(-1, step_back.shape[2]), seq_slot, axis=0)
    gated = mix_sequence(
        seq_gate,
        seq_state,
        seq_step,
        conv_weight,
        conv_bias,
        step_bias,
        decay_log,
        skip_gain,
        HEAD_DIM,
    )
    owner = (
        jnp.full((experts * shards * capacity,), length, jnp.int32)
        .at[seq_slot]
        .set(jnp.arange(length, dtype=jnp.int32))
    )
    leaving = jnp.take(gated, owner, axis=0, mode="fill", fill_value=0).reshape(
        experts, shards * capacity, chans
    )
    returned = lax.all_to_all(leaving, "expert", split_axis=0, concat_axis=0, tiled=True)
    parts = jnp.dot(
        returned.reshape(-1, chans), w_out[0], preferred_element_type=jnp.float32
    ).astype(jnp.bfloat16)
    parts = parts.reshape(experts, shards, capacity, width)
    pieces = lax.all_to_all(
        lax.all_to_all(parts, "expert", split_axis=0, concat_axis=0, tiled=True),
        "context",
        split_axis=1,
        concat_axis=1,
        tiled=True,
    )
    summed = jnp.sum(pieces.astype(jnp.float32), axis=1).astype(jnp.bfloat16)
    result = jnp.take(summed.reshape(-1, width), local_slot, axis=0)
    return result[None]


def solution(mesh):
    in_specs = (
        P("expert", "context", None),
        P("expert", None, None),
        P("expert", None, None, "context"),
        P("expert", None, None),
        P("expert", None, "context"),
        P("context"),
        P("context"),
        P("context"),
        P(None, "context"),
        P("context"),
        P("expert", "context", None),
    )
    out_specs = P("expert", "context", None)
    return jax.shard_map(
        per_device, mesh=mesh, in_specs=in_specs, out_specs=out_specs, check_vma=False
    )
```

profile of v0, /device:TPU:7, one launch (start us, length us, event | category | flops | bytes accessed | tf_op | source)
XLA Modules:
  0.0 722.5 jit_solution(15315165236449053569)
XLA Ops:
  8.2 2.5 select_reduce_fusion
  11.0 1.5 fusion.39
  12.4 35.7 %all_to_all.35 = bf16[32,8,2048]{2,1,0:T(8,128)(2,1)} all-to-all(bf16[32,8,2048]{2,1,0:T(8,128)(2,1)S(1)} %fusion.39), channel_id=1, replica_groups=mesh['expert'=32,'context'=8] {'expert'}, dimensions={0} | all-to-all | bytes 2097152 | tf_op jit(solution)/shard_map/all_to_all | solution.py:126
  48.2 5.4 copy.150
  53.6 46.4 %all-gather.2.cloned.1.call-done = bf16[32,64,2048]{2,1,0:T(8,128)(2,1)} async-done(((bf16[32,8,2048]{2,1,0:T(8,128)(2,1)}), bf16[32,64,2048]{2,1,0:T(8,128)(2,1)}) %all-gather.2.cloned.1.call-update) | async-done | bytes 8388624 | tf_op jit(solution)/shard_map/all_gather | solution.py:127
  100.0 5.7 convolution_convert_fusion.4
  106.6 9.7 %all-to-all-start.1 = ((bf16[32,2,256]{2,1,0:T(2,128)(2,1)}), bf16[32,2,256]{2,1,0:T(2,128)(2,1)S(1)}, u32[]{:S(2)}, u32[]{:S(2)}) async-start(bf16[32,2,256]{2,1,0:T(2,128)(2,1)} %reshape.335), calls=%async_computation.1 | async-start | bytes 65536 | tf_op jit(solution)/shard_map/all_to_all | solution.py:140
  116.3 6.5 convolution_convert_fusion.3
  122.8 2.2 all-to-all-done.1
  125.0 7.2 all-to-all-start.3
  132.2 13.8 %convolution_convert_fusion.1 = bf16[2048,1024]{1,0:T(8,128)(2,1)} fusion(bf16[2048,2048]{1,0:T(8,128)(2,1)} %bitcast.168, bf16[2048,1024]{1,0:T(8,128)(2,1)} %bitcast.177), kind=kOutput, calls=%fused_computation.54 | convolution fusion | flops 8592031744 | bytes 16777216 | tf_op jit(solution)/shard_map/dot_general | solution.py:129
  146.1 9.3 %all-to-all-start.2 = ((bf16[32,64,1024]{2,1,0:T(8,128)(2,1)}), bf16[32,64,1024]{2,1,0:T(8,128)(2,1)}, u32[]{:S(2)}, u32[]{:S(2)}) async-start(bf16[32,64,1024]{2,1,0:T(8,128)(2,1)} %bitcast.176), calls=%async_computation.2 | async-start | bytes 8388608 | tf_op jit(solution)/shard_map/all_to_all | solution.py:138
  155.6 4.3 scatter_custom_fusion
  160.6 4.3 gather_fusion
  166.0 3.2 gather_fusion.2
  169.9 82.1 %all-to-all-done.2 = bf16[32,64,1024]{2,1,0:T(8,128)(2,1)} async-done(((bf16[32,64,1024]{2,1,0:T(8,128)(2,1)}), bf16[32,64,1024]{2,1,0:T(8,128)(2,1)}, u32[]{:S(2)}, u32[]{:S(2)}) %all-to-all-start.2) | async-done | bytes 4194336 | tf_op jit(solution)/shard_map/all_to_all | solution.py:138
  252.0 8.8 %gather_fusion.1 = bf16[1024,1024]{1,0:T(8,128)(2,1)} fusion(bf16[2048,1024]{1,0:T(8,128)(2,1)} %bitcast.18, s32[1024]{0:T(1024)S(1)} %broadcast_clamp_fusion), kind=kCustom, calls=%fused_computation.1 | custom fusion | bytes 4198400 | tf_op jit(solution)/shard_map/jit(_take)/gather | solution.py:147
  260.8 1.9 bitcast_select_fusion
  265.6 2.6 divide_multiply_fusion
  268.2 4.4 reshape.328
  272.6 3.8 copy.136
  276.5 45.0 %while.13 = (s32[]{:T(128)}, f32[8,64,64]{2,1,0:T(8,128)S(1)}, f32[8,128,8,64]{1,3,2,0:T(8,128)}, f32[8,128,8]{1,2,0:T(8,128)S(1)}, f32[8,128,8]{1,2,0:T(8,128)S...) while((s32[]{:T(128)}, f32[8,64,64]{2,1,0:T(8,128)S(1)}, ...), condition=%wide.region_5.6_spmd.clone, body=%wide.region_3.5_spmd.clone.sunk | while | flops 214909952 | bytes 2367776 | solution.py:64
  277.1 2.1 convolution_bitcast_fusion.2
  280.6 1.5 convolution_add_fusion.2
  282.8 2.1 convolution_bitcast_fusion.2
  286.2 1.5 convolution_add_fusion.2
  288.4 2.1 convolution_bitcast_fusion.2
  291.9 1.5 convolution_add_fusion.2
  294.0 2.1 convolution_bitcast_fusion.2
  299.7 2.1 convolution_bitcast_fusion.2
  305.3 2.1 convolution_bitcast_fusion.2
  308.7 1.5 convolution_add_fusion.2
  310.9 2.1 convolution_bitcast_fusion.2
  316.5 2.1 convolution_bitcast_fusion.2
  321.5 3.9 copy.144
  325.3 4.8 reshape.329
  330.1 5.8 fusion.47
  335.9 9.2 %gather_fusion.3 = bf16[2048,512]{1,0:T(8,128)(2,1)} fusion(bf16[1024,512]{1,0:T(8,128)(2,1)S(1)} %fusion.47, s32[2048]{0:T(1024)S(1)} %fusion.56), kind=kCustom, calls=%fused_computation.3 | custom fusion | bytes 4202496 | tf_op jit(solution)/shard_map/jit(_take)/gather | solution.py:168
  345.1 1.8 broadcast_select_fusion
  346.9 52.6 %all_to_all.36 = bf16[32,64,512]{2,1,0:T(8,128)(2,1)S(1)} all-to-all(bf16[32,64,512]{2,1,0:T(8,128)(2,1)S(1)} %broadcast_select_fusion), channel_id=1, replica_groups=mesh['expert'=32,'context'=8] {'expert'}, dimensions={0} | all-to-all | bytes 4194304 | tf_op jit(solution)/shard_map/all_to_all | solution.py:171
  399.5 4.7 convolution_convert_fusion
  404.3 190.5 %all_to_all.37 = bf16[32,8,8,2048]{3,2,1,0:T(8,128)(2,1)} all-to-all(bf16[32,8,8,2048]{3,2,1,0:T(8,128)(2,1)S(1)} %bitcast.173), channel_id=1, replica_groups=mesh['expert'=32,'context'=8] {'expert'}, dimensions={0} | all-to-all | bytes 16777216 | tf_op jit(solution)/shard_map/all_to_all | solution.py:177
  594.8 8.3 %copy.141 = bf16[32,8,8,2048]{3,2,0,1:T(8,128)(2,1)} copy(bf16[32,8,8,2048]{3,2,1,0:T(8,128)(2,1)} %all_to_all.37) | data formatting | bytes 16777216 | tf_op jit(solution)/shard_map/all_to_all | solution.py:177
  603.1 11.6 %all-to-all-start.6 = ((bf16[32,8,8,2048]{3,2,0,1:T(8,128)(2,1)}), bf16[32,8,8,2048]{3,2,0,1:T(8,128)(2,1)}, u32[]{:S(2)}, u32[]{:S(2)}) async-start(bf16[32,8,8,2048]{3,2,0,1:T(8,128)(2,1)} %copy.141), calls=%async_computation.6 | async-start | bytes 16777216 | tf_op jit(solution)/shard_map/all_to_all | solution.py:176
  614.7 92.1 %all-to-all-done.6 = bf16[32,8,8,2048]{3,2,0,1:T(8,128)(2,1)} async-done(((bf16[32,8,8,2048]{3,2,0,1:T(8,128)(2,1)}), bf16[32,8,8,2048]{3,2,0,1:T(8,128)(2,1)}, u32[]{:S(2)}, u32[]{:S(2)}) %all-to-all-start.6) | async-done | bytes 8388640 | tf_op jit(solution)/shard_map/all_to_all | solution.py:176
  706.8 5.2 reduce_sum.28
  712.0 1.7 gather_fusion.4
  713.7 1.9 bitcast_select_fusion.1
  (169 shorter events, 29.9 us)
Async XLA Ops:
  6.5 393.0 %copy-start = (bf16[1,512,2048]{2,1,0:T(8,128)(2,1)S(1)}, bf16[1,512,2048]{2,1,0:T(8,128)(2,1)}, u32[]{:S(2)}) copy-start(bf16[1,512,2048]{2,1,0:T(8,128)(2,1)} %param.23) | copy-start | bytes 6291460
  6.5 93.4 %all-gather.2.cloned.1.call-start = ((), (), s32[]{:S(2)}) async-start(), calls=%async_computation.7 | async-start | bytes 9437184 | tf_op jit(solution)/shard_map/all_gather | solution.py:127
  48.2 51.8 %copy-start.4 = (bf16[1,2048,8]{1,2,0:T(8,128)(2,1)S(1)}, bf16[1,2048,8]{1,2,0:T(8,128)(2,1)}, u32[]{:S(2)}) copy-start(bf16[1,2048,8]{1,2,0:T(8,128)(2,1)} %param.17) | copy-start | bytes 98308
  100.0 16.3 %copy-start.9 = (bf16[1,2048,128]{2,1,0:T(8,128)(2,1)S(1)}, bf16[1,2048,128]{2,1,0:T(8,128)(2,1)}, u32[]{:S(2)}) copy-start(bf16[1,2048,128]{2,1,0:T(8,128)(2,1)} %param.16) | copy-start | bytes 1572868
  106.6 18.5 %all-to-all-start.1 = ((bf16[32,2,256]{2,1,0:T(2,128)(2,1)}), bf16[32,2,256]{2,1,0:T(2,128)(2,1)S(1)}, u32[]{:S(2)}, u32[]{:S(2)}) async-start(bf16[32,2,256]{2,1,0:T(2,128)(2,1)} %reshape.335), calls=%async_computation.1 | async-start | bytes 65536 | tf_op jit(solution)/shard_map/all_to_all | solution.py:140
  125.0 21.0 %all-to-all-start.3 = ((bf16[32,64,128]{2,1,0:T(8,128)(2,1)}), bf16[32,64,128]{2,1,0:T(8,128)(2,1)S(1)}, u32[]{:S(2)}, u32[]{:S(2)}) async-start(bf16[32,64,128]{2,1,0:T(8,128)(2,1)} %bitcast.25), calls=%async_computation.3 | async-start | bytes 1048576 | tf_op jit(solution)/shard_map/all_to_all | solution.py:139
  146.1 9.4 %copy-start.8 = (f32[8]{0:T(128)S(1)}, f32[8]{0:T(128)}, u32[]{:S(2)}) copy-start(f32[8]{0:T(128)} %param.20) | copy-start | bytes 100
  146.1 9.5 %copy-start.3 = (s32[1,1024,1]{1,2,0:T(1,128)S(1)}, s32[1,1024,1]{1,2,0:T(1,128)}, u32[]{:S(2)}) copy-start(s32[1,1024,1]{1,2,0:T(1,128)} %param.14) | copy-start | bytes 12292
  146.1 14.0 %copy-start.10 = (f32[8]{0:T(128)S(1)}, f32[8]{0:T(128)}, u32[]{:S(2)}) copy-start(f32[8]{0:T(128)} %param.19) | copy-start | bytes 100
  146.1 14.1 %copy-start.6 = (f32[4,512]{1,0:T(4,128)S(1)}, f32[4,512]{1,0:T(4,128)}, u32[]{:S(2)}) copy-start(f32[4,512]{1,0:T(4,128)} %param.21) | copy-start | bytes 24580
  146.1 105.9 %all-to-all-start.2 = ((bf16[32,64,1024]{2,1,0:T(8,128)(2,1)}), bf16[32,64,1024]{2,1,0:T(8,128)(2,1)}, u32[]{:S(2)}, u32[]{:S(2)}) async-start(bf16[32,64,1024]{2,1,0:T(8,128)(2,1)} %bitcast.176), calls=%async_computation.2 | async-start | bytes 8388608 | tf_op jit(solution)/shard_map/all_to_all | solution.py:138
  155.4 10.6 %copy-start.7 = (f32[8]{0:T(128)S(1)}, f32[8]{0:T(128)}, u32[]{:S(2)}) copy-start(f32[8]{0:T(128)} %param.18) | copy-start | bytes 100
  262.7 1.3 copy-start.2
  264.0 1.6 copy-start.5
  264.3 1.3 copy-start.1
  603.1 103.7 %all-to-all-start.6 = ((bf16[32,8,8,2048]{3,2,0,1:T(8,128)(2,1)}), bf16[32,8,8,2048]{3,2,0,1:T(8,128)(2,1)}, u32[]{:S(2)}, u32[]{:S(2)}) async-start(bf16[32,8,8,2048]{3,2,0,1:T(8,128)(2,1)} %copy.141), calls=%async_computation.6 | async-start | bytes 16777216 | tf_op jit(solution)/shard_map/all_to_all | solution.py:176
Sparse Core Ops, SparseCore 0:
  48.3 51.5 all-gather.1
where the time goes:
time: 726 us; the launch traced here: 722 us
  blocking collectives  279 us (38%)
  waiting for transfers between devices  223 us (31%)
  matrix products  72 us (10%)
  local copies, waits for them, and re-layouts  71.5 us (10%)
  starting transfers between devices  37.7 us (5%)
  other arithmetic  25.2 us (3%)
  between operations  13.7 us (2%)
    all_to_all x1, blocking collectives, per_device(): lax.all_to_all(parts, 'expert', split_axis=0, concat_axis=0, tiled=True)  191 us
    all_to_all x1, waiting for transfers between devices, per_device(): lax.all_to_all(lax.all_to_all(parts, 'expert', split_axis=0, concat_axis=...  92.1 us
    all_to_all x1, waiting for transfers between devices, per_device(): lax.all_to_all(gate_inner, 'expert', split_axis=0, concat_axis=0, tiled=T...  82.1 us
    all_to_all x1, blocking collectives, per_device(): lax.all_to_all(leaving, 'expert', split_axis=0, concat_axis=0, tiled=True)  52.6 us
    all_gather x1, waiting for transfers between devices, per_device(): gathered = lax.all_gather(arrived, 'context', axis=1, tiled=True)  46.4 us
    all_to_all x1, blocking collectives, per_device(): lax.all_to_all(outgoing, 'expert', split_axis=0, concat_axis=0, tiled=True)  35.7 us
    dot_general x8, matrix products, advance(): local = jnp.einsum('tuh,uhp->thp', weights, values, precision=exact)  17.1 us
  transfers between devices with their start and end apart: 5, of which 5 were waited for; matrix products, arithmetic and copies ran while one was open for 6% of the time, Pallas kernels for 0%

commit v1 on v0

v1 whole, which is shorter than its diff:
```python
import functools

import jax
import jax.numpy as jnp
from jax import lax
from jax.experimental import pallas as pl
from jax.experimental.pallas import tpu as pltpu
from jax.sharding import PartitionSpec as P

HEAD_DIM = 64
MESH = pl.DeviceIdType.MESH
F32 = jnp.float32
BF16 = jnp.bfloat16
VMEM_LIMIT = 60 * 1024 * 1024


def _dot(a, b, dims=((1,), (0,)), precision=None):
    return lax.dot_general(a, b, (dims, ((), ())), precision=precision, preferred_element_type=F32)


def _meet(expert_peers, context_peers):
    e, c = lax.axis_index("expert"), lax.axis_index("context")
    barrier = pltpu.get_barrier_semaphore()

    def greet(axis, me, count):
        def body(k, carry):
            peer = lax.rem(me + k, count)
            pl.semaphore_signal(barrier, inc=1, device_id={axis: peer}, device_id_type=MESH)
            return carry

        lax.fori_loop(1, count, body, 0)

    greet("expert", e, expert_peers)
    greet("context", c, context_peers)
    pl.semaphore_wait(barrier, expert_peers + context_peers - 2)


def _drain(ref, sem):
    pltpu.make_async_copy(ref, ref, sem).wait()


def _fold(top, bottom):
    n, w = top.shape[0] // 8, top.shape[1]
    return jnp.concatenate([top.reshape(n, 8, w), bottom.reshape(n, 8, w)], axis=1).astype(BF16)


def _unfold(folded):
    n, _, w = folded.shape
    wide = folded.astype(F32)
    return (
        wide[:, :8, :].reshape(n * 8, w).astype(BF16),
        wide[:, 8:, :].reshape(n * 8, w).astype(BF16),
    )


def _scatter_expert(E, src, dst, send_sem, recv_sem):
    e = lax.axis_index("expert")

    def body(k, carry):
        peer = lax.rem(e + k, E)
        pltpu.make_async_remote_copy(
            src_ref=src.at[peer],
            dst_ref=dst.at[e],
            send_sem=send_sem,
            recv_sem=recv_sem,
            device_id={"expert": peer},
            device_id_type=MESH,
        ).start()
        return carry

    lax.fori_loop(1, E, body, 0)
    dst[e] = src[e]


def _slot_onehot(row, n, half):
    place = row + (row & -8) + 8 * half
    return (lax.broadcasted_iota(jnp.int32, (n, row.shape[1]), 0) == place).astype(BF16)


def project_kernel(
    E,
    C,
    slots,
    tokens,
    w_inner_hbm,
    w_state,
    w_step,
    gate_out,
    inner_out,
    ss_out,
    w_inner,
    stok,
    rtok,
    rows,
    sinner,
    wstep_all,
    sss,
    rss,
    tok_sem,
    ss_sem,
    inner_send,
    inner_recv,
    row_send,
    row_recv,
    fwd_send,
    step_send,
    step_recv,
    pos_send,
    pos_recv,
    w_sem,
):
    e, c = lax.axis_index("expert"), lax.axis_index("context")
    x, core = c // 2, lax.rem(c, 2)
    sibling = c + 1 - 2 * core
    chips = C // 2
    width = tokens.shape[1]
    half = width // 2
    chans = inner_out.shape[3]
    nrow = E * 8

    load_w = pltpu.make_async_copy(w_inner_hbm, w_inner, w_sem)
    load_w.start()

    row = slots[pl.ds(c, 1), :]
    dispatch = (lax.broadcasted_iota(jnp.int32, (nrow, row.shape[1]), 0) == row).astype(BF16)
    for part in range(2):
        cols = slice(part * half // 2, (part + 1) * half // 2)
        late = slice(half + part * half // 2, half + (part + 1) * half // 2)
        stok[:, :, cols] = _fold(_dot(dispatch, tokens[:, cols]), _dot(dispatch, tokens[:, late]))
    heads = w_step.shape[0]
    wide = w_step[...].astype(F32)
    wstep_all[c] = jnp.concatenate([wide, jnp.zeros((16 - heads, width), F32)], axis=0).astype(BF16)

    _meet(E, C)
    _scatter_expert(E, stok, rtok, tok_sem.at[0], tok_sem.at[1])

    def share(ref, send_sem, recv_sem):
        def body(k, carry):
            peer = lax.rem(c + k, C)
            pltpu.make_async_remote_copy(
                src_ref=ref.at[c],
                dst_ref=ref.at[c],
                send_sem=send_sem,
                recv_sem=recv_sem,
                device_id={"context": peer},
                device_id_type=MESH,
            ).start()
            return carry

        lax.fori_loop(1, C, body, 0)

    share(wstep_all, step_send, step_recv)

    _drain(rtok.at[pl.ds(0, E - 1)], tok_sem.at[1])
    for part in range(2):
        cols = slice(part * half // 2, (part + 1) * half // 2)
        late = slice(half + part * half // 2, half + (part + 1) * half // 2)
        left, right = _unfold(rtok[:, :, cols])
        rows[c, :, cols] = left
        rows[c, :, late] = right

    def send_rows(block, target, send_sem):
        return pltpu.make_async_remote_copy(
            src_ref=rows.at[block],
            dst_ref=rows.at[block],
            send_sem=send_sem,
            recv_sem=row_recv.at[block],
            device_id={"context": target},
            device_id_type=MESH,
        )

    for k in range(1, chips):
        send_rows(c, lax.rem(x + k, chips) * 2 + core, row_send.at[k]).start()
    send_rows(c, sibling, row_send.at[0]).start()

    _drain(wstep_all.at[pl.ds(0, C - 1)], step_recv)
    state = _dot(rows[c], w_state[...])
    step = _dot(rows[c], wstep_all[...].reshape(C * 16, width), ((1,), (1,)))
    both = jnp.concatenate([state, step], axis=1)
    sss[...] = _fold(both, jnp.zeros_like(both))
    _scatter_expert(E, sss, rss, ss_sem.at[0], ss_sem.at[1])

    def project(chip):
        pair = rows[pl.ds(chip * 2, 2)].reshape(2 * nrow, width)
        step_n = min(256, chans)
        for n in range(chans // step_n):
            cols = slice(n * step_n, (n + 1) * step_n)
            there = slice(chans + n * step_n, chans + (n + 1) * step_n)
            res = _dot(pair, w_inner[:, there])
            sinner[chip, :, :, cols] = _fold(res[:nrow], res[nrow:])
        _scatter_expert(E, sinner.at[chip], inner_out.at[chip], inner_send.at[chip], inner_recv.at[chip])
        for n in range(chans // step_n):
            cols = slice(n * step_n, (n + 1) * step_n)
            res = _dot(pair, w_inner[:, cols])
            gate_out[chip, :, :, cols] = _fold(res[:nrow], res[nrow:])

    load_w.wait()
    _drain(rows.at[0], row_recv.at[sibling])
    project(x)

    _drain(rss.at[pl.ds(0, E - 1)], ss_sem.at[1])
    here = _slot_onehot(row, E * 16, 0)
    ss_out[c] = _dot(here, rss[...].reshape(E * 16, rss.shape[2]), ((0,), (0,))).astype(BF16)
    share(ss_out, pos_send, pos_recv)

    def remote_chip(i, carry):
        far = 1 + 2 * i - 3 * (i // 2)
        chip = lax.rem(x + far, chips)
        block = chip * 2 + core
        _drain(rows.at[0], row_recv.at[block])
        send_rows(block, sibling, fwd_send.at[i]).start()
        _drain(rows.at[0], row_recv.at[chip * 2 + 1 - core])
        project(chip)
        return carry

    lax.fori_loop(0, chips - 1, remote_chip, 0)

    _drain(ss_out.at[pl.ds(0, C - 1)], pos_recv)
    for chip in range(chips):
        _drain(inner_out.at[chip, pl.ds(0, E - 1)], inner_recv.at[chip])
    _drain(stok.at[pl.ds(0, E - 1)], tok_sem.at[0])
    _drain(sss.at[pl.ds(0, E - 1)], ss_sem.at[0])
    _drain(wstep_all.at[pl.ds(0, C - 1)], step_send)
    _drain(ss_out.at[pl.ds(0, C - 1)], pos_send)
    for chip in range(chips):
        _drain(sinner.at[chip, pl.ds(0, E - 1)], inner_send.at[chip])
        _drain(rows.at[0], row_send.at[chip])
        if chip < chips - 1:
            _drain(rows.at[0], fwd_send.at[chip])


def scan_kernel(
    E,
    C,
    slots,
    inner,
    ss,
    conv_weight,
    conv_bias,
    per_lane,
    per_row,
    skip,
    back_out,
    state,
    tail8,
    scanned,
    sback,
    send_sem,
    recv_sem,
):
    c = lax.axis_index("context")
    exact = lax.Precision.HIGHEST
    T = slots.shape[1]
    chans = inner.shape[3]
    heads = chans // HEAD_DIM
    taps = conv_weight.shape[0]
    nbc = HEAD_DIM

    _meet(E, 1)

    state[...] = jnp.zeros_like(state)
    tail8[...] = jnp.zeros_like(tail8)
    at0 = lax.broadcasted_iota(jnp.int32, (T, T), 0)
    at1 = lax.broadcasted_iota(jnp.int32, (T, T), 1)
    lower = at0 >= at1
    lower_one = lower.astype(F32)
    upper_one = (at0 <= at1).astype(F32)
    lane = lax.broadcasted_iota(jnp.int32, (T, 2 * HEAD_DIM), 1)
    first = lane < HEAD_DIM
    lanes = C * 16
    pick = (
        lax.broadcasted_iota(jnp.int32, (lanes, 128), 0)
        == c * 16 + lax.broadcasted_iota(jnp.int32, (lanes, 128), 1)
    ) & (lax.broadcasted_iota(jnp.int32, (lanes, 128), 1) < heads)
    pick = pick.astype(BF16)
    pick_t = (
        lax.broadcasted_iota(jnp.int32, (16, lanes), 1)
        == c * 16 + lax.broadcasted_iota(jnp.int32, (16, lanes), 0)
    ).astype(BF16)
    bias_l, rate_l = per_lane[0:1, :], -jnp.exp(per_lane[1:2, :])
    bias_r, rate_r = per_row[:, 0:1], -jnp.exp(per_row[:, 1:2])

    def softplus(v):
        return jnp.maximum(v, 0.0) + jnp.log1p(jnp.exp(-jnp.abs(v)))

    def chunk(b, half):
        bp = b // 2
        row = slots[pl.ds(b, 1), :]
        place = _slot_onehot(row, E * 16, half)
        raw = _dot(place, inner[bp].reshape(E * 16, chans), ((0,), (0,)))
        joined = jnp.concatenate([tail8[...], raw], axis=0)
        tail8[...] = raw[T - 8 :, :]
        conv = conv_bias[...] + jnp.zeros_like(raw)
        for j in range(taps):
            begin = 8 - taps + 1 + j
            conv = conv + conv_weight[j : j + 1, :] * joined[begin : begin + T, :]
        signal = conv * jax.nn.sigmoid(conv)

        mine = ss[b]
        keys, queries = mine[:, :nbc], mine[:, nbc : 2 * nbc]
        raw_step = mine[:, 2 * nbc :]
        steps = softplus(_dot(raw_step, pick) + bias_l)
        steps_t = softplus(_dot(pick_t, raw_step, ((1,), (1,))) + bias_r)
        summed = _dot(lower_one, steps * rate_l, precision=exact)
        summed_t = _dot(steps_t * rate_r, upper_one, precision=exact)
        scores = _dot(queries, keys, ((1,), (1,)))
        grown = jnp.exp(summed)
        end = summed[T - 1 : T, :]
        tail = jnp.exp(end - summed) * steps
        whole = jnp.exp(end)
        for pair in range(heads // 2):
            cols = slice(pair * 2 * HEAD_DIM, (pair + 1) * 2 * HEAD_DIM)
            xs = signal[:, cols]
            xb = xs.astype(BF16)
            weights = []
            for h in (2 * pair, 2 * pair + 1):
                gaps = summed[:, h : h + 1] - summed_t[h : h + 1, :]
                decay = jnp.exp(jnp.where(lower, gaps, -jnp.inf))
                weights.append((scores * decay * steps_t[h : h + 1, :]).astype(BF16))
            zero = jnp.zeros_like(xb)
            stacked = jnp.concatenate([jnp.where(first, xb, zero), jnp.where(first, zero, xb)], axis=0)
            local = _dot(jnp.concatenate(weights, axis=1), stacked)

            def spread(v, n):
                a = jnp.broadcast_to(v[:, 2 * pair : 2 * pair + 1], (n, 2 * HEAD_DIM))
                z = jnp.broadcast_to(v[:, 2 * pair + 1 : 2 * pair + 2], (n, 2 * HEAD_DIM))
                return jnp.where(first[:n], a, z)

            old = state[:, cols]
            carried = spread(grown, T) * _dot(queries, old.astype(BF16))
            fed = (spread(tail, T) * xs).astype(BF16)
            state[:, cols] = spread(whole, 1) * old + _dot(keys, fed, ((0,), (0,)))
            scanned[half, :, cols] = (local + carried + skip[:, cols] * xs).astype(BF16)

    def pair_of_chunks(bp, carry):
        chunk(2 * bp, 0)
        chunk(2 * bp + 1, 1)
        total = None
        for half in range(2):
            row = slots[pl.ds(2 * bp + half, 1), :]
            term = _dot(_slot_onehot(row, E * 16, half), scanned[half])
            total = term if total is None else total + term
        sback[bp] = total.astype(BF16).reshape(E, 16, chans)
        _scatter_expert(E, sback.at[bp], back_out.at[bp], send_sem.at[bp], recv_sem.at[bp])
        return carry

    lax.fori_loop(0, C // 2, pair_of_chunks, 0)
    for chip in range(C // 2):
        _drain(back_out.at[chip, pl.ds(0, E - 1)], recv_sem.at[chip])
    for chip in range(C // 2):
        _drain(sback.at[chip, pl.ds(0, E - 1)], send_sem.at[chip])


def mix_kernel(
    E,
    C,
    slots,
    back,
    gate,
    w_out_hbm,
    out,
    w_out,
    gated,
    kept,
    sib_src,
    sib_dst,
    far_src,
    far_dst,
    fin_src,
    fin_dst,
    sib_send,
    sib_recv,
    far_send,
    far_recv,
    fin_send,
    fin_recv,
    w_sem,
):
    c = lax.axis_index("context")
    x, core = c // 2, lax.rem(c, 2)
    sibling = c + 1 - 2 * core
    chips = C // 2
    nrow = E * 8
    parts, _, _, step_n = kept.shape
    chans = back.shape[3]

    load_w = pltpu.make_async_copy(w_out_hbm, w_out, w_sem)
    load_w.start()
    for chip in range(chips):
        g = gate[chip].astype(F32)
        v = back[chip].astype(F32) * (g * jax.nn.sigmoid(g))
        gated[chip] = v.astype(BF16)
    _meet(E, C)
    load_w.wait()

    for j in range(parts):

        def emit(chip, carry):
            rows = gated[chip].reshape(2 * nrow, chans)
            part = _dot(rows, w_out[:, j * step_n : (j + 1) * step_n])
            part = part.reshape(E, 2, 8, step_n)
            both = jnp.stack([part[:, 0].reshape(nrow, step_n), part[:, 1].reshape(nrow, step_n)])
            kept[j, chip] = jnp.where(core == 0, both[0], both[1]).astype(BF16)
            sib_src[j, chip] = jnp.where(core == 0, both[1], both[0]).astype(BF16)
            return carry

        lax.fori_loop(0, chips, emit, 0)
        pltpu.make_async_remote_copy(
            src_ref=sib_src.at[j],
            dst_ref=sib_dst.at[j],
            send_sem=sib_send.at[j],
            recv_sem=sib_recv.at[j],
            device_id={"context": sibling},
            device_id_type=MESH,
        ).start()

    def far_copy(j, k):
        chip = lax.rem(x + k, chips)
        return pltpu.make_async_remote_copy(
            src_ref=far_src.at[j, k - 1],
            dst_ref=far_dst.at[j, k - 1],
            send_sem=far_send.at[j, k - 1],
            recv_sem=far_recv.at[j, k - 1],
            device_id={"context": chip * 2 + core},
            device_id_type=MESH,
        )

    for j in range(parts):
        _drain(sib_dst.at[j], sib_recv.at[j])

        def forward(k, carry):
            chip = lax.rem(x + k, chips)
            both = kept[j, chip].astype(F32) + sib_dst[j, chip].astype(F32)
            far_src[j, k - 1] = both.astype(BF16)
            far_copy(j, k).start()
            return carry

        lax.fori_loop(1, chips, forward, 0)

    for j in range(parts):
        total = kept[j, x].astype(F32) + sib_dst[j, x].astype(F32)
        for k in range(1, chips):
            _drain(far_dst.at[j, k - 1], far_recv.at[j, k - 1])
            total = total + far_dst[j, k - 1].astype(F32)
        fin_src[j] = _fold(total[:, : step_n // 2], total[:, step_n // 2 :])
        _scatter_expert(E, fin_src.at[j], fin_dst.at[j], fin_send.at[j], fin_recv.at[j])

    row = slots[pl.ds(c, 1), :]
    places = [_slot_onehot(row, E * 16, half) for half in range(2)]
    for j in range(parts):
        _drain(fin_dst.at[j, pl.ds(0, E - 1)], fin_recv.at[j])
        arrived = fin_dst[j].reshape(E * 16, step_n // 2)
        for half in range(2):
            begin = j * step_n + half * (step_n // 2)
            res = _dot(places[half], arrived, ((0,), (0,)))
            out[:, begin : begin + step_n // 2] = res.astype(BF16)

    for j in range(parts):
        _drain(sib_src.at[j], sib_send.at[j])
        _drain(fin_src.at[j, pl.ds(0, E - 1)], fin_send.at[j])
        for k in range(1, chips):
            _drain(far_src.at[j, k - 1], far_send.at[j, k - 1])


def per_device(
    tokens,
    route,
    w_inner,
    w_state,
    w_step,
    step_bias,
    decay_log,
    skip_gain,
    conv_weight,
    conv_bias,
    w_out,
):
    T, width = tokens.shape[1:]
    E, C = lax.axis_size("expert"), lax.axis_size("context")
    chips = C // 2
    chans = w_inner.shape[3]
    heads = w_step.shape[2]
    nboth = w_state.shape[2]
    ids = route[0, :, 0].reshape(C, T)
    same = ids[:, :, None] == ids[:, None, :]
    before = jnp.arange(T)[None, :] < jnp.arange(T)[:, None]
    ranks = jnp.sum((same & before[None]).astype(jnp.int32), axis=2)
    slots = ids * 8 + ranks

    vmem = pl.BlockSpec(memory_space=pltpu.VMEM)
    hbm = pl.BlockSpec(memory_space=pl.ANY)
    dma = pltpu.SemaphoreType.DMA
    flat = jax.ShapeDtypeStruct((chips, E, 16, chans), BF16)

    def params(number):
        return pltpu.CompilerParams(
            collective_id=number, has_side_effects=True, vmem_limit_bytes=VMEM_LIMIT
        )

    wide = nboth + C * 16
    gate, inner, ss = pl.pallas_call(
        functools.partial(project_kernel, E, C),
        out_shape=(flat, flat, jax.ShapeDtypeStruct((C, T, wide), BF16)),
        in_specs=[vmem, vmem, hbm, vmem, vmem],
        out_specs=(vmem, vmem, vmem),
        scratch_shapes=[
            pltpu.VMEM((width, 2 * chans), BF16),
            pltpu.VMEM((E, 16, width // 2), BF16),
            pltpu.VMEM((E, 16, width // 2), BF16),
            pltpu.VMEM((C, E * 8, width), BF16),
            pltpu.VMEM((chips, E, 16, chans), BF16),
            pltpu.VMEM((C, 16, width), BF16),
            pltpu.VMEM((E, 16, wide), BF16),
            pltpu.VMEM((E, 16, wide), BF16),
            dma((2,)),
            dma((2,)),
            dma((chips,)),
            dma((chips,)),
            dma((chips,)),
            dma((C,)),
            dma((chips,)),
            dma,
            dma,
            dma,
            dma,
            dma,
        ],
        compiler_params=params(0),
        name="project",
    )(slots, tokens[0], w_inner[0].reshape(width, 2 * chans), w_state[0], w_step[0].T)

    pad = 128 - heads
    per_lane = jnp.pad(jnp.stack([step_bias, decay_log]), ((0, 0), (0, pad)))
    per_row = jnp.pad(jnp.stack([step_bias, decay_log], axis=1), ((0, 16 - heads), (0, 0)))
    back = pl.pallas_call(
        functools.partial(scan_kernel, E, C),
        out_shape=flat,
        in_specs=[vmem] * 8,
        out_specs=vmem,
        scratch_shapes=[
            pltpu.VMEM((HEAD_DIM, chans), F32),
            pltpu.VMEM((8, chans), F32),
            pltpu.VMEM((2, T, chans), BF16),
            pltpu.VMEM((chips, E, 16, chans), BF16),
            dma((chips,)),
            dma((chips,)),
        ],
        compiler_params=params(1),
        name="scan",
    )(
        slots,
        inner,
        ss,
        conv_weight,
        conv_bias[None, :],
        per_lane,
        per_row,
        jnp.repeat(skip_gain, HEAD_DIM)[None, :],
    )

    parts = 4
    step_n = width // parts
    blocks = (parts, chips, E * 8, step_n)
    fars = (parts, chips - 1, E * 8, step_n)
    fins = (parts, E, 16, step_n // 2)
    mixed = pl.pallas_call(
        functools.partial(mix_kernel, E, C),
        out_shape=jax.ShapeDtypeStruct((T, width), BF16),
        in_specs=[vmem, vmem, vmem, hbm],
        out_specs=vmem,
        scratch_shapes=[
            pltpu.VMEM((chans, width), BF16),
            pltpu.VMEM((chips, E, 16, chans), BF16),
            pltpu.VMEM(blocks, BF16),
            pltpu.VMEM(blocks, BF16),
            pltpu.VMEM(blocks, BF16),
            pltpu.VMEM(fars, BF16),
            pltpu.VMEM(fars, BF16),
            pltpu.VMEM(fins, BF16),
            pltpu.VMEM(fins, BF16),
            dma((parts,)),
            dma((parts,)),
            dma((parts, chips - 1)),
            dma((parts, chips - 1)),
            dma((parts,)),
            dma((parts,)),
            dma,
        ],
        compiler_params=params(2),
        name="mix",
    )(slots, back, gate, w_out[0])
    return mixed[None]


def solution(mesh):
    in_specs = (
        P("expert", "context", None),
        P("expert", None, None),
        P("expert", None, None, "context"),
        P("expert", None, None),
        P("expert", None, "context"),
        P("context"),
        P("context"),
        P("context"),
        P(None, "context"),
        P("context"),
        P("expert", "context", None),
    )
    out_specs = P("expert", "context", None)
    return jax.shard_map(
        per_device, mesh=mesh, in_specs=in_specs, out_specs=out_specs, check_vma=False
    )
```

time: 726 us -> 270 us (0.37)
  blocking collectives: 279 us -> 0 us
  Pallas kernels: 0 us -> 255 us
  waiting for transfers between devices: 223 us -> 0 us
  matrix products: 72 us -> 0 us
  local copies, waits for them, and re-layouts: 71.5 us -> 8.63 us
  starting transfers between devices: 37.7 us -> 0 us
  other arithmetic: 25.2 us -> 2.97 us
  between operations: 13.7 us -> 0.06 us
    all_to_all x3 -> x0, blocking collectives: 279 us -> none  [the longest x1 191 us: per_device(): lax.all_to_all(parts, 'expert', split_axis=0, concat_axis=0, tiled=True)]
    pallas_call x0 -> x3, Pallas kernels: none -> 255 us  [the longest x1 125 us: per_device(): pl.pallas_call(functools.partial(project_kernel, E, C), out_shape=(flat,...]
    all_to_all x4 -> x0, waiting for transfers between devices: 177 us -> none  [the longest x1 92.1 us: per_device(): lax.all_to_all(lax.all_to_all(parts, 'expert', split_axis=0, concat_axis=...]
    dot_general x37 -> x0, matrix products: 72 us -> none  [the longest x8 17.1 us: advance(): local = jnp.einsum('tuh,uhp->thp', weights, values, precision=exact)]
    all_gather x1 -> x0, waiting for transfers between devices: 46.4 us -> none  [per_device(): gathered = lax.all_gather(arrived, 'context', axis=1, tiled=True)]
    all_to_all x4 -> x0, starting transfers between devices: 37.7 us -> none  [the longest x1 11.6 us: per_device(): lax.all_to_all(lax.all_to_all(parts, 'expert', split_axis=0, concat_axis=...]
    gather x6 -> x0, local copies, waits for them, and re-layouts: 28.3 us -> none  [the longest x1 9.19 us: per_device(): jnp.take(gated, owner, axis=0, mode='fill', fill_value=0)]
    reshape x4 -> x0, local copies, waits for them, and re-layouts: 8.81 us -> none  [the longest x2 8.64 us: state_scan(): return outputs.reshape(length, heads, head_dim)]
  transfers between devices with their start and end apart: 5 -> 0, of which waited for: 5 -> 0; matrix products, arithmetic and copies ran while one was open for 6% -> 0% of each run, Pallas kernels for 0% -> 0%
where the time goes in v1:
time: 270 us; the launch traced here: 266 us
  Pallas kernels  255 us (94%)
  local copies, waits for them, and re-layouts  8.63 us (3%)
  other arithmetic  2.97 us (1%)
    pallas_call x1, Pallas kernels, per_device(): pl.pallas_call(functools.partial(project_kernel, E, C), out_shape=(flat,...  125 us
    pallas_call x1, Pallas kernels, per_device(): pl.pallas_call(functools.partial(mix_kernel, E, C), out_shape=jax.ShapeDt...  70.9 us
    pallas_call x1, Pallas kernels, per_device(): pl.pallas_call(functools.partial(scan_kernel, E, C), out_shape=flat, in_s...  58.3 us
    unnamed x8, local copies, waits for them, and re-layouts  7.2 us

profile of v1, /device:TPU:7, one launch (start us, length us, event | category | flops | bytes accessed | tf_op | source)
XLA Modules:
  0.0 266.3 jit_solution(14914778615205351988)
XLA Ops:
  0.0 1.1 convert_reduce_fusion
  1.2 1.3 multiply_add_fusion.slots
  2.4 5.3 %copy.16 = bf16[256,8,2,512]{3,1,2,0:T(8,128)(2,1)} copy(bf16[256,8,2,512]{3,2,1,0:T(2,128)(2,1)} %bitcast.17) | data formatting | bytes 8388608
  7.7 0.0 copy-start
  7.8 0.0 copy-start.1
  7.8 0.0 copy-start.2
  7.8 125.4 %project.1 = (bf16[4,32,16,512]{3,2,1,0:T(8,128)(2,1)}, bf16[4,32,16,512]{3,2,1,0:T(8,128)(2,1)}, bf16[8,128,256]{2,1,0:T(8,128)(2,1)}) custom-call(s32[8,128]{1,0:T(8,128)} %multiply_add_fusion.slots, bf16[128,2048]{1,0:T(8,128)(2,1)} %bitcast.20, bf16[2048,1024]{1,0:T(8,128)(2,1)} %bitcast.16, bf16[2048,128]{1,0:T(8,128)(2,1)} %bitcast.21, ...), custom_call_target="tpu_custom_call" | custom-call | tf_op jit(solution)/shard_map/project/pallas_call | solution.py:501
  133.2 0.0 copy-done
  133.2 0.0 copy-done.1
  133.2 0.1 copy.15
  133.3 0.6 pad.9.per_row
  133.9 0.0 copy-done.2
  133.9 0.1 broadcast_in_dim.13
  134.0 0.7 broadcast_in_dim_reshape.3.skip
  134.7 0.5 select_maximum_fusion.per_lane
  135.2 58.3 %scan.1.back = bf16[4,32,16,512]{3,2,1,0:T(8,128)(2,1)} custom-call(s32[8,128]{1,0:T(8,128)} %multiply_add_fusion.slots, bf16[4,32,16,512]{3,2,1,0:T(8,128)(2,1)} %get-tuple-element.8.inner, bf16[8,128,256]{2,1,0:T(8,128)(2,1)} %get-tuple-element.9.ss, f32[4,512]{1,0:T(4,128)} %conv_weight.1, f32[1,512]{1,0:T(1,128)} %bitcast.25, ...), custom_call_target="tpu_custom_call" | custom-call | tf_op jit(solution)/shard_map/scan/pallas_call | solution.py:535
  193.5 70.9 %mix.1 = bf16[128,2048]{1,0:T(8,128)(2,1)} custom-call(s32[8,128]{1,0:T(8,128)} %multiply_add_fusion.slots, bf16[4,32,16,512]{3,2,1,0:T(8,128)(2,1)} %scan.1.back, bf16[4,32,16,512]{3,2,1,0:T(8,128)(2,1)} %get-tuple-element.10.gate, bf16[512,2048]{1,0:T(8,128)(2,1)} %bitcast.18), custom_call_target="tpu_custom_call" | custom-call | tf_op jit(solution)/shard_map/mix/pallas_call | solution.py:566
  264.5 1.9 copy.18
  (2 shorter events, 0.0 us)
Async XLA Ops:
  7.7 125.5 %copy-start = (f32[8]{0:T(128)S(1)}, f32[8]{0:T(128)}, u32[]{:S(2)}) copy-start(f32[8]{0:T(128)} %param.17) | copy-start | bytes 100
  7.8 125.5 %copy-start.1 = (f32[8]{0:T(128)S(1)}, f32[8]{0:T(128)}, u32[]{:S(2)}) copy-start(f32[8]{0:T(128)} %param.16) | copy-start | bytes 100
  7.8 126.2 %copy-start.2 = (f32[8]{0:T(128)S(1)}, f32[8]{0:T(128)}, u32[]{:S(2)}) copy-start(f32[8]{0:T(128)} %param.18) | copy-start | bytes 100

commit v2 on v0

v2 whole, which is shorter than its diff:
```python
import functools

import jax
import jax.numpy as jnp
from jax import lax
from jax.experimental import pallas as pl
from jax.experimental.pallas import tpu as pltpu
from jax.sharding import PartitionSpec as P

HEAD_DIM = 64
MESH = pl.DeviceIdType.MESH
F32 = jnp.float32
BF16 = jnp.bfloat16
VMEM_LIMIT = 60 * 1024 * 1024


def _dot(a, b, dims=((1,), (0,)), precision=None):
    return lax.dot_general(a, b, (dims, ((), ())), precision=precision, preferred_element_type=F32)


def _meet(expert_peers, context_peers):
    e, c = lax.axis_index("expert"), lax.axis_index("context")
    barrier = pltpu.get_barrier_semaphore()

    def greet(axis, me, count):
        def body(k, carry):
            peer = lax.rem(me + k, count)
            pl.semaphore_signal(barrier, inc=1, device_id={axis: peer}, device_id_type=MESH)
            return carry

        lax.fori_loop(1, count, body, 0)

    greet("expert", e, expert_peers)
    greet("context", c, context_peers)
    pl.semaphore_wait(barrier, expert_peers + context_peers - 2)


def _drain(ref, sem):
    pltpu.make_async_copy(ref, ref, sem).wait()


def _fold(top, bottom):
    n, w = top.shape[0] // 8, top.shape[1]
    return jnp.concatenate([top.reshape(n, 8, w), bottom.reshape(n, 8, w)], axis=1).astype(BF16)


def _unfold(folded):
    n, _, w = folded.shape
    wide = folded.astype(F32)
    return (
        wide[:, :8, :].reshape(n * 8, w).astype(BF16),
        wide[:, 8:, :].reshape(n * 8, w).astype(BF16),
    )


def _scatter_expert(E, src, dst, send_sem, recv_sem):
    e = lax.axis_index("expert")

    def body(k, carry):
        peer = lax.rem(e + k, E)
        pltpu.make_async_remote_copy(
            src_ref=src.at[peer],
            dst_ref=dst.at[e],
            send_sem=send_sem,
            recv_sem=recv_sem,
            device_id={"expert": peer},
            device_id_type=MESH,
        ).start()
        return carry

    lax.fori_loop(1, E, body, 0)
    dst[e] = src[e]


def _slot_onehot(row, n, half):
    place = row + (row & -8) + 8 * half
    return (lax.broadcasted_iota(jnp.int32, (n, row.shape[1]), 0) == place).astype(BF16)


def _remote(src, dst, send_sem, recv_sem, **where):
    return pltpu.make_async_remote_copy(
        src_ref=src,
        dst_ref=dst,
        send_sem=send_sem,
        recv_sem=recv_sem,
        device_id=where,
        device_id_type=MESH,
    )


def _softplus(v):
    return jnp.maximum(v, 0.0) + jnp.log1p(jnp.exp(-jnp.abs(v)))


def _iota(shape, axis):
    return lax.broadcasted_iota(jnp.int32, shape, axis)


def layer_kernel(
    E,
    C,
    ids,
    tokens,
    w_inner_hbm,
    w_state,
    w_step,
    step_bias,
    decay_log,
    skip_gain,
    conv_weight,
    conv_bias,
    w_out_hbm,
    out,
    slots,
    w3,
    w_inner,
    w_out,
    stok,
    rtok,
    rows,
    sinner,
    inner,
    gate,
    sback,
    back,
    wstep_all,
    sss,
    rss,
    ss,
    gathered,
    fin_src,
    fin_dst,
    state,
    tail8,
    scanned,
    w3_sem,
    w_sem,
    tok_send,
    tok_recv,
    step_send,
    step_recv,
    row_send,
    row_recv,
    fwd_send,
    hop_send,
    ss_send,
    ss_recv,
    pos_send,
    pos_recv,
    inner_send,
    inner_recv,
    wout_send,
    wout_recv,
    back_send,
    back_recv,
    gated_send,
    gated_recv,
    fin_send,
    fin_recv,
):
    e, c = lax.axis_index("expert"), lax.axis_index("context")
    x, core = c // 2, lax.rem(c, 2)
    sibling = c + 1 - 2 * core
    chips = C // 2
    T, width = tokens.shape
    half = width // 2
    quarter = width // 4
    chans = inner.shape[3]
    nrow = E * 8
    nslot = E * 16
    heads = w_step.shape[0]
    pieces, piece = w3.shape[0], w3.shape[1]
    count = width // piece
    early = w_out.shape[1] // 8
    peers = pl.ds(0, E - 1)

    def load_piece(q):
        return pltpu.make_async_copy(
            w_inner_hbm.at[pl.ds(q * piece, piece)], w3.at[q % pieces], w3_sem.at[q % pieces]
        )

    for q in range(pieces):
        load_piece(q).start()
    load_w_out = pltpu.make_async_copy(w_out_hbm, w_out.at[c], w_sem)
    load_w_out.start()

    values = ids[...].astype(F32)
    eye = (_iota((T, T), 0) == _iota((T, T), 1)).astype(BF16)
    columns = _dot(eye, values.astype(BF16), ((1,), (1,)))
    earlier = _iota((T, T), 0) < _iota((T, T), 1)
    for b in range(C):
        same = (columns[:, b : b + 1] == values[b : b + 1, :]) & earlier
        rank = jnp.sum(same.astype(F32), axis=0, keepdims=True)
        slots[b : b + 1, :] = ids[b : b + 1, :] * 8 + rank.astype(jnp.int32)

    row = slots[pl.ds(c, 1), :]
    dispatch = (_iota((nrow, T), 0) == row).astype(BF16)

    def pack(h):
        a = h * half
        stok[h] = _fold(
            _dot(dispatch, tokens[:, a : a + quarter]),
            _dot(dispatch, tokens[:, a + quarter : a + half]),
        )

    pack(0)
    _meet(E, C)
    _scatter_expert(E, stok.at[0], rtok.at[0], tok_send.at[0], tok_recv.at[0])
    pack(1)
    _scatter_expert(E, stok.at[1], rtok.at[1], tok_send.at[1], tok_recv.at[1])

    def share(ref, send_sem, recv_sem):
        def body(k, carry):
            peer = lax.rem(c + k, C)
            _remote(ref.at[c], ref.at[c], send_sem, recv_sem, context=peer).start()
            return carry

        lax.fori_loop(1, C, body, 0)

    wide = w_step[...].astype(F32)
    wstep_all[c] = jnp.concatenate([wide, jnp.zeros((16 - heads, width), F32)], axis=0).astype(BF16)
    share(wstep_all, step_send, step_recv)

    def send_w_out(k, part):
        where = pl.ds(0, early) if part == 0 else pl.ds(early, w_out.shape[1] - early)
        return _remote(
            w_out.at[c, where],
            w_out.at[c, where],
            wout_send.at[part, k],
            wout_recv.at[part, c],
            context=lax.rem(x + k, chips) * 2 + core,
        )

    load_w_out.wait()
    for k in range(1, chips):
        send_w_out(k, 0).start()

    for q in range(count):
        load_piece(q).wait()

        def part_w(i, carry):
            block = w3[q % pieces, pl.ds(i * 128, 128)]
            at = pl.ds(pl.multiple_of(q * piece + i * 128, 128), 128)
            w_inner[0, at, :] = block[:, 0, :]
            w_inner[1, at, :] = block[:, 1, :]
            return carry

        lax.fori_loop(0, piece // 128, part_w, 0)
        if q + pieces < count:
            load_piece(q + pieces).start()

    right = lax.rem(x + 1, chips) * 2 + core
    left = lax.rem(x + chips - 1, chips) * 2 + core
    across = lax.rem(x + chips // 2, chips) * 2 + core

    def send_rows(h, block, target, sem):
        return _remote(rows.at[h, block], rows.at[h, block], sem, row_recv.at[h, block], context=target)

    def await_rows(h, block):
        _drain(rows.at[h, block], row_recv.at[h, block])

    for h in range(2):
        _drain(rtok.at[h, peers], tok_recv.at[h])
        first_q, second_q = _unfold(rtok[h])
        rows[h, c, :, :quarter] = first_q
        rows[h, c, :, quarter:] = second_q
        send_rows(h, c, right, row_send.at[h, 0]).start()
        send_rows(h, c, left, row_send.at[h, 1]).start()
        send_rows(h, c, sibling, row_send.at[h, 2]).start()

    _drain(wstep_all.at[pl.ds(0, C - 1)], step_recv)
    both = []
    for h in range(2):
        mine = rows[h, c]
        at = slice(h * half, (h + 1) * half)
        step_w = wstep_all[:, :, at].reshape(C * 16, half)
        both.append(
            jnp.concatenate([_dot(mine, w_state[at, :]), _dot(mine, step_w, ((1,), (1,)))], axis=1)
        )
    vectors = both[0] + both[1]
    sss[...] = _fold(vectors, jnp.zeros_like(vectors))
    _scatter_expert(E, sss, rss, ss_send, ss_recv)

    step_n = min(256, chans)

    def project(chip, which, dst):
        first = rows[0, pl.ds(chip * 2, 2)].reshape(2 * nrow, half)
        second = rows[1, pl.ds(chip * 2, 2)].reshape(2 * nrow, half)
        for n in range(chans // step_n):
            cols = slice(n * step_n, (n + 1) * step_n)
            res = _dot(first, w_inner[which, :half, cols]) + _dot(second, w_inner[which, half:, cols])
            dst[chip, :, :, cols] = _fold(res[:nrow], res[nrow:])

    def inner_chip(i, carry):
        chip = lax.rem(x + i + i // 2 - 2 * (i // 3), chips)

        @pl.when(i == 1)
        def _():
            await_rows(0, left)
            send_rows(0, left, right, hop_send.at[0]).start()
            send_rows(0, left, sibling, fwd_send.at[0, 0]).start()
            await_rows(0, right)
            send_rows(0, right, sibling, fwd_send.at[0, 1]).start()
            await_rows(1, right)
            send_rows(1, right, left, hop_send.at[1]).start()
            send_rows(1, right, sibling, fwd_send.at[1, 1]).start()
            await_rows(1, left)
            send_rows(1, left, sibling, fwd_send.at[1, 0]).start()

        @pl.when(i == chips - 1)
        def _():
            for h in range(2):
                await_rows(h, across)
                send_rows(h, across, sibling, fwd_send.at[h, 2]).start()

        for h in range(2):
            await_rows(h, chip * 2 + 1 - core)
        project(chip, 1, sinner)
        _scatter_expert(E, sinner.at[chip], inner.at[chip], inner_send.at[chip], inner_recv.at[chip])
        return carry

    lax.fori_loop(0, chips, inner_chip, 0)

    _remote(w_out.at[c], w_out.at[c], wout_send.at[0, 0], wout_recv.at[2, c], context=sibling).start()
    send_w_out(1, 1).start()
    send_w_out(chips - 1, 1).start()

    _drain(rss.at[peers], ss_recv)
    here = _slot_onehot(row, nslot, 0)
    ss[c] = _dot(here, rss[...].reshape(nslot, rss.shape[2]), ((0,), (0,))).astype(BF16)
    share(ss, pos_send, pos_recv)

    def gate_chip(chip, carry):
        project(chip, 0, gate)
        return carry

    lax.fori_loop(0, chips, gate_chip, 0)

    exact = lax.Precision.HIGHEST
    taps = conv_weight.shape[0]
    nbc = HEAD_DIM
    state[...] = jnp.zeros_like(state)
    tail8[...] = jnp.zeros_like(tail8)
    lower = _iota((T, T), 0) >= _iota((T, T), 1)
    lower_one = lower.astype(F32)
    upper_one = (_iota((T, T), 0) <= _iota((T, T), 1)).astype(F32)
    first = _iota((T, 2 * HEAD_DIM), 1) < HEAD_DIM
    lanes = C * 16
    pick = (_iota((lanes, heads), 0) == c * 16 + _iota((lanes, heads), 1)).astype(BF16)
    pick_t = (_iota((heads, lanes), 1) == c * 16 + _iota((heads, lanes), 0)).astype(BF16)
    diagonal = _iota((heads, heads), 0) == _iota((heads, heads), 1)

    def column(v):
        return jnp.sum(jnp.where(diagonal, v, 0.0), axis=1, keepdims=True)

    bias_l, rate_l = step_bias[...], -jnp.exp(decay_log[...])
    bias_r, rate_r = column(bias_l), column(rate_l)
    gain = skip_gain[...]

    def chunk(b, part):
        place = _slot_onehot(slots[pl.ds(b, 1), :], nslot, part)
        raw = _dot(place, inner[b // 2].reshape(nslot, chans), ((0,), (0,)))
        joined = jnp.concatenate([tail8[...], raw], axis=0)
        tail8[...] = raw[T - 8 :, :]
        conv = conv_bias[...] + jnp.zeros_like(raw)
        for j in range(taps):
            begin = 8 - taps + 1 + j
            conv = conv + conv_weight[j : j + 1, :] * joined[begin : begin + T, :]
        signal = conv * jax.nn.sigmoid(conv)

        mine = ss[b]
        keys, queries = mine[:, :nbc], mine[:, nbc : 2 * nbc]
        raw_step = mine[:, 2 * nbc :]
        steps = _softplus(_dot(raw_step, pick) + bias_l)
        steps_t = _softplus(_dot(pick_t, raw_step, ((1,), (1,))) + bias_r)
        summed = _dot(lower_one, steps * rate_l, precision=exact)
        summed_t = _dot(steps_t * rate_r, upper_one, precision=exact)
        scores = _dot(queries, keys, ((1,), (1,)))
        grown = jnp.exp(summed)
        end = summed[T - 1 : T, :]
        tail = jnp.exp(end - summed) * steps
        whole = jnp.exp(end)
        for pair in range(heads // 2):
            cols = slice(pair * 2 * HEAD_DIM, (pair + 1) * 2 * HEAD_DIM)
            xs = signal[:, cols]
            xb = xs.astype(BF16)
            weights = []
            for h in (2 * pair, 2 * pair + 1):
                gaps = summed[:, h : h + 1] - summed_t[h : h + 1, :]
                decay = jnp.exp(jnp.where(lower, gaps, -jnp.inf))
                weights.append((scores * decay * steps_t[h : h + 1, :]).astype(BF16))
            zero = jnp.zeros_like(xb)
            stacked = jnp.concatenate([jnp.where(first, xb, zero), jnp.where(first, zero, xb)], axis=0)
            local = _dot(jnp.concatenate(weights, axis=1), stacked)

            def spread(v):
                n = v.shape[0]
                a = jnp.broadcast_to(v[:, 2 * pair : 2 * pair + 1], (n, 2 * HEAD_DIM))
                z = jnp.broadcast_to(v[:, 2 * pair + 1 : 2 * pair + 2], (n, 2 * HEAD_DIM))
                return jnp.where(first[:n], a, z)

            old = state[:, cols]
            carried = spread(grown) * _dot(queries, old.astype(BF16))
            fed = (spread(tail) * xs).astype(BF16)
            state[:, cols] = spread(whole) * old + _dot(keys, fed, ((0,), (0,)))
            scanned[part, :, cols] = (local + carried + spread(gain) * xs).astype(BF16)

    _drain(ss.at[pl.ds(0, C - 1)], pos_recv)

    def pair_of_chunks(bp, carry):
        _drain(inner.at[bp, peers], inner_recv.at[bp])
        chunk(2 * bp, 0)
        chunk(2 * bp + 1, 1)
        total = None
        for part in range(2):
            place = _slot_onehot(slots[pl.ds(2 * bp + part, 1), :], nslot, part)
            term = _dot(place, scanned[part])
            total = term if total is None else total + term
        sback[bp] = total.astype(BF16).reshape(E, 16, chans)
        _scatter_expert(E, sback.at[bp], back.at[bp], back_send.at[bp], back_recv.at[bp])

        @pl.when(bp == 1)
        def _():
            send_w_out(2, 1).start()

        return carry

    lax.fori_loop(0, chips, pair_of_chunks, 0)

    def forward_w_out(block, k):
        pltpu.make_async_copy(
            w_out.at[block, pl.ds(0, early)], w_out.at[block, pl.ds(0, early)], wout_recv.at[0, block]
        ).wait()
        rest = pl.ds(early, w_out.shape[1] - early)
        pltpu.make_async_copy(
            w_out.at[block, rest], w_out.at[block, rest], wout_recv.at[1, block]
        ).wait()
        _remote(
            w_out.at[block], w_out.at[block], wout_send.at[1, 0] if k == 0 else fwd_send.at[k - 1, 3],
            wout_recv.at[2, block], context=sibling,
        ).start()

    forward_w_out(right, 0)
    forward_w_out(left, 1)

    for chip in range(chips):
        _drain(sinner.at[chip, peers], inner_send.at[chip])

    def gate_rows(bp, carry):
        _drain(back.at[bp, peers], back_recv.at[bp])
        g = gate[bp].astype(F32)
        v = back[bp].astype(F32) * (g * jax.nn.sigmoid(g))
        for part in range(2):
            mine = v[:, part * 8 : (part + 1) * 8, :].reshape(nslot // 2, chans).astype(BF16)
            at = pl.ds(part * (E // 2), E // 2)
            sinner[bp, at] = mine.reshape(E // 2, 16, chans)
            target = 2 * bp + part

            @pl.when(target != c)
            def _():
                _remote(
                    sinner.at[bp, at],
                    gathered.at[c],
                    gated_send.at[target],
                    gated_recv.at[c],
                    context=target,
                ).start()

            @pl.when(target == c)
            def _():
                gathered[c] = mine.reshape(E // 2, 16, chans)

        return carry

    lax.fori_loop(0, chips, gate_rows, 0)
    forward_w_out(across, 2)

    for k in range(1, C):
        block = lax.rem(c + k, C)
        _drain(gathered.at[block], gated_recv.at[block])
    for k in range(chips):
        block = lax.rem(x + k, chips) * 2 + 1 - core
        _drain(w_out.at[block], wout_recv.at[2, block])
    parts, _, _, fin_n = fin_src.shape

    def finish(j, carry):
        total = jnp.zeros((nrow, 2 * fin_n), F32)
        cols = pl.ds(pl.multiple_of(j * 2 * fin_n, 2 * fin_n), 2 * fin_n)
        for block in range(C):
            total = total + _dot(gathered[block].reshape(nrow, chans), w_out[block, :, cols])
        fin_src[j] = _fold(total[:, :fin_n], total[:, fin_n:])
        _scatter_expert(E, fin_src.at[j], fin_dst.at[j], fin_send.at[j], fin_recv.at[j])
        return carry

    lax.fori_loop(0, parts, finish, 0)

    places = [_slot_onehot(row, nslot, part) for part in range(2)]
    for j in range(parts):
        _drain(fin_dst.at[j, peers], fin_recv.at[j])
        arrived = fin_dst[j].reshape(nslot, fin_n)
        for part in range(2):
            begin = (2 * j + part) * fin_n
            out[:, begin : begin + fin_n] = _dot(places[part], arrived, ((0,), (0,))).astype(BF16)

    for h in range(2):
        _drain(stok.at[h, peers], tok_send.at[h])
        for k in range(3):
            _drain(rows.at[h, 0], row_send.at[h, k])
            _drain(rows.at[h, 0], fwd_send.at[h, k])
        _drain(rows.at[h, 0], hop_send.at[h])
    _drain(wstep_all.at[pl.ds(0, C - 1)], step_send)
    _drain(sss.at[peers], ss_send)
    _drain(ss.at[pl.ds(0, C - 1)], pos_send)
    for chip in range(chips):
        _drain(sback.at[chip, peers], back_send.at[chip])
    for k in range(1, C):
        target = lax.rem(c + k, C)
        _drain(gathered.at[0], gated_send.at[target])
    for j in range(parts):
        _drain(fin_src.at[j, peers], fin_send.at[j])
    for k in range(1, chips):
        _drain(w_out.at[0, pl.ds(0, early)], wout_send.at[0, k])
        _drain(w_out.at[0, pl.ds(early, w_out.shape[1] - early)], wout_send.at[1, k])
    _drain(w_out.at[0], wout_send.at[0, 0])
    _drain(w_out.at[0], wout_send.at[1, 0])
    _drain(w_out.at[0], fwd_send.at[0, 3])
    _drain(w_out.at[0], fwd_send.at[1, 3])


def per_device(
    tokens,
    route,
    w_inner,
    w_state,
    w_step,
    step_bias,
    decay_log,
    skip_gain,
    conv_weight,
    conv_bias,
    w_out,
):
    T, width = tokens.shape[1:]
    E, C = lax.axis_size("expert"), lax.axis_size("context")
    chips = C // 2
    chans = w_inner.shape[3]
    wide = w_state.shape[2] + C * 16
    parts = 4
    fin_n = width // parts // 2
    vmem = pl.BlockSpec(memory_space=pltpu.VMEM)
    hbm = pl.BlockSpec(memory_space=pl.ANY)
    dma = pltpu.SemaphoreType.DMA
    flat = pltpu.VMEM((chips, E, 16, chans), BF16)
    mixed = pl.pallas_call(
        functools.partial(layer_kernel, E, C),
        out_shape=jax.ShapeDtypeStruct((T, width), BF16),
        in_specs=[vmem, vmem, hbm, vmem, vmem, vmem, vmem, vmem, vmem, vmem, hbm],
        out_specs=vmem,
        scratch_shapes=[
            pltpu.VMEM((C, T), jnp.int32),
            pltpu.VMEM((2, width // 4, 2, chans), BF16),
            pltpu.VMEM((2, width, chans), BF16),
            pltpu.VMEM((C, chans, width), BF16),
            pltpu.VMEM((2, E, 16, width // 4), BF16),
            pltpu.VMEM((2, E, 16, width // 4), BF16),
            pltpu.VMEM((2, C, E * 8, width // 2), BF16),
            flat,
            flat,
            flat,
            flat,
            flat,
            pltpu.VMEM((C, 16, width), BF16),
            pltpu.VMEM((E, 16, wide), BF16),
            pltpu.VMEM((E, 16, wide), BF16),
            pltpu.VMEM((C, T, wide), BF16),
            pltpu.VMEM((C, E // 2, 16, chans), BF16),
            pltpu.VMEM((parts, E, 16, fin_n), BF16),
            pltpu.VMEM((parts, E, 16, fin_n), BF16),
            pltpu.VMEM((HEAD_DIM, chans), F32),
            pltpu.VMEM((8, chans), F32),
            pltpu.VMEM((2, T, chans), BF16),
            dma((2,)),
            dma,
            dma((2,)),
            dma((2,)),
            dma,
            dma,
            dma((2, 3)),
            dma((2, C)),
            dma((2, 4)),
            dma((2,)),
            dma,
            dma,
            dma,
            dma,
            dma((chips,)),
            dma((chips,)),
            dma((2, chips)),
            dma((3, C)),
            dma((chips,)),
            dma((chips,)),
            dma((C,)),
            dma((C,)),
            dma((parts,)),
            dma((parts,)),
        ],
        compiler_params=pltpu.CompilerParams(
            collective_id=0, has_side_effects=True, vmem_limit_bytes=VMEM_LIMIT
        ),
        name="layer",
    )(
        route[0, :, 0].reshape(C, T),
        tokens[0],
        w_inner[0],
        w_state[0],
        w_step[0].T,
        step_bias[None, :],
        decay_log[None, :],
        skip_gain[None, :],
        conv_weight,
        conv_bias[None, :],
        w_out[0],
    )
    return mixed[None]


def solution(mesh):
    in_specs = (
        P("expert", "context", None),
        P("expert", None, None),
        P("expert", None, None, "context"),
        P("expert", None, None),
        P("expert", None, "context"),
        P("context"),
        P("context"),
        P("context"),
        P(None, "context"),
        P("context"),
        P("expert", "context", None),
    )
    out_specs = P("expert", "context", None)
    return jax.shard_map(
        per_device, mesh=mesh, in_specs=in_specs, out_specs=out_specs, check_vma=False
    )
```

time: 726 us -> 220 us (0.30)
  blocking collectives: 279 us -> 0 us
  waiting for transfers between devices: 223 us -> 0 us
  Pallas kernels: 0 us -> 218 us
  matrix products: 72 us -> 0 us
  local copies, waits for them, and re-layouts: 71.5 us -> 1.88 us
  starting transfers between devices: 37.7 us -> 0 us
  other arithmetic: 25.2 us -> 0 us
  between operations: 13.7 us -> 0.01 us
    all_to_all x3 -> x0, blocking collectives: 279 us -> none  [the longest x1 191 us: per_device(): lax.all_to_all(parts, 'expert', split_axis=0, concat_axis=0, tiled=True)]
    pallas_call x0 -> x1, Pallas kernels: none -> 218 us  [per_device(): pl.pallas_call(functools.partial(layer_kernel, E, C), out_shape=jax.Shape...]
    all_to_all x4 -> x0, waiting for transfers between devices: 177 us -> none  [the longest x1 92.1 us: per_device(): lax.all_to_all(lax.all_to_all(parts, 'expert', split_axis=0, concat_axis=...]
    dot_general x37 -> x0, matrix products: 72 us -> none  [the longest x8 17.1 us: advance(): local = jnp.einsum('tuh,uhp->thp', weights, values, precision=exact)]
    all_gather x1 -> x0, waiting for transfers between devices: 46.4 us -> none  [per_device(): gathered = lax.all_gather(arrived, 'context', axis=1, tiled=True)]
    all_to_all x4 -> x0, starting transfers between devices: 37.7 us -> none  [the longest x1 11.6 us: per_device(): lax.all_to_all(lax.all_to_all(parts, 'expert', split_axis=0, concat_axis=...]
    gather x6 -> x0, local copies, waits for them, and re-layouts: 28.3 us -> none  [the longest x1 9.19 us: per_device(): jnp.take(gated, owner, axis=0, mode='fill', fill_value=0)]
    unnamed x28 -> x1, local copies, waits for them, and re-layouts: 12.9 us -> 1.88 us
  transfers between devices with their start and end apart: 5 -> 0, of which waited for: 5 -> 0; matrix products, arithmetic and copies ran while one was open for 6% -> 0% of each run, Pallas kernels for 0% -> 0%
where the time goes in v2:
time: 220 us
  Pallas kernels  218 us (99%)
    pallas_call x1, Pallas kernels, per_device(): pl.pallas_call(functools.partial(layer_kernel, E, C), out_shape=jax.Shape...  218 us

profile of v2, /device:TPU:7, one launch (start us, length us, event | category | flops | bytes accessed | tf_op | source)
XLA Modules:
  0.0 219.7 jit_solution(15641469033428615803)
XLA Ops:
  0.0 217.8 %layer.1 = bf16[128,2048]{1,0:T(8,128)(2,1)} custom-call(s32[8,128]{1,0:T(8,128)} %bitcast.19, bf16[128,2048]{1,0:T(8,128)(2,1)} %bitcast.16, bf16[2048,2,512]{2,1,0:T(2,128)(2,1)} %bitcast.13, bf16[2048,128]{1,0:T(8,128)(2,1)} %bitcast.17, bf16[8,2048]{1,0:T(8,128)(2,1)} %bitcast.18, f32[1,8]{1,0:T(1,128)} %bitcast.21, f32[1,8]{1,0:T(1,128)} %bitcast.22, ...), custom_call_target="tpu_custom_call" | custom-call | tf_op jit(solution)/shard_map/layer/pallas_call | solution.py:554
  217.8 1.9 copy.13

commit v3 on v2

--- a/solution.py
+++ b/solution.py
@@ -18,7 +18,7 @@
     return lax.dot_general(a, b, (dims, ((), ())), precision=precision, preferred_element_type=F32)
 
 
-def _meet(expert_peers, context_peers):
+def _greet(expert_peers, context_peers):
     e, c = lax.axis_index("expert"), lax.axis_index("context")
     barrier = pltpu.get_barrier_semaphore()
 
@@ -32,7 +32,10 @@
 
     greet("expert", e, expert_peers)
     greet("context", c, context_peers)
-    pl.semaphore_wait(barrier, expert_peers + context_peers - 2)
+
+
+def _meet(expert_peers, context_peers):
+    pl.semaphore_wait(pltpu.get_barrier_semaphore(), expert_peers + context_peers - 2)
 
 
 def _drain(ref, sem):
@@ -171,7 +174,8 @@
     heads = w_step.shape[0]
     pieces, piece = w3.shape[0], w3.shape[1]
     count = width // piece
-    early = w_out.shape[1] // 8
+    depth = w_out.shape[1]
+    early = depth // 16 * 5
     peers = pl.ds(0, E - 1)
 
     def load_piece(q):
@@ -179,6 +183,7 @@
             w_inner_hbm.at[pl.ds(q * piece, piece)], w3.at[q % pieces], w3_sem.at[q % pieces]
         )
 
+    _greet(E, C)
     for q in range(pieces):
         load_piece(q).start()
     load_w_out = pltpu.make_async_copy(w_out_hbm, w_out.at[c], w_sem)
@@ -221,19 +226,22 @@
     wstep_all[c] = jnp.concatenate([wide, jnp.zeros((16 - heads, width), F32)], axis=0).astype(BF16)
     share(wstep_all, step_send, step_recv)
 
-    def send_w_out(k, part):
-        where = pl.ds(0, early) if part == 0 else pl.ds(early, w_out.shape[1] - early)
+    right = lax.rem(x + 1, chips) * 2 + core
+    left = lax.rem(x + chips - 1, chips) * 2 + core
+    across = lax.rem(x + chips // 2, chips) * 2 + core
+
+    def send_w_out(block, where, target, sem, kind):
         return _remote(
-            w_out.at[c, where],
-            w_out.at[c, where],
-            wout_send.at[part, k],
-            wout_recv.at[part, c],
-            context=lax.rem(x + k, chips) * 2 + core,
+            w_out.at[block, where], w_out.at[block, where], sem, wout_recv.at[kind, block], context=target
         )
 
+    def await_w_out(block, where, kind):
+        _drain(w_out.at[block, where], wout_recv.at[kind, block])
+
+    first_part, last_part, all_parts = pl.ds(0, early), pl.ds(early, depth - early), pl.ds(0, depth)
     load_w_out.wait()
-    for k in range(1, chips):
-        send_w_out(k, 0).start()
+    send_w_out(c, first_part, right, wout_send.at[0], 0).start()
+    send_w_out(c, first_part, left, wout_send.at[1], 0).start()
 
     for q in range(count):
         load_piece(q).wait()
@@ -248,10 +256,6 @@
         lax.fori_loop(0, piece // 128, part_w, 0)
         if q + pieces < count:
             load_piece(q + pieces).start()
-
-    right = lax.rem(x + 1, chips) * 2 + core
-    left = lax.rem(x + chips - 1, chips) * 2 + core
-    across = lax.rem(x + chips // 2, chips) * 2 + core
 
     def send_rows(h, block, target, sem):
         return _remote(rows.at[h, block], rows.at[h, block], sem, row_recv.at[h, block], context=target)
@@ -268,19 +272,6 @@
         send_rows(h, c, left, row_send.at[h, 1]).start()
         send_rows(h, c, sibling, row_send.at[h, 2]).start()
 
-    _drain(wstep_all.at[pl.ds(0, C - 1)], step_recv)
-    both = []
-    for h in range(2):
-        mine = rows[h, c]
-        at = slice(h * half, (h + 1) * half)
-        step_w = wstep_all[:, :, at].reshape(C * 16, half)
-        both.append(
-            jnp.concatenate([_dot(mine, w_state[at, :]), _dot(mine, step_w, ((1,), (1,)))], axis=1)
-        )
-    vectors = both[0] + both[1]
-    sss[...] = _fold(vectors, jnp.zeros_like(vectors))
-    _scatter_expert(E, sss, rss, ss_send, ss_recv)
-
     step_n = min(256, chans)
 
     def project(chip, which, dst):
@@ -291,44 +282,61 @@
             res = _dot(first, w_inner[which, :half, cols]) + _dot(second, w_inner[which, half:, cols])
             dst[chip, :, :, cols] = _fold(res[:nrow], res[nrow:])
 
-    def inner_chip(i, carry):
-        chip = lax.rem(x + i + i // 2 - 2 * (i // 3), chips)
+    def inner_chip(chip):
+        for h in range(2):
+            await_rows(h, chip * 2 + 1 - core)
+        project(chip, 1, sinner)
+        _scatter_expert(E, sinner.at[chip], inner.at[chip], inner_send.at[chip], inner_recv.at[chip])
+
+    await_rows(0, left)
+    send_rows(0, left, right, hop_send.at[0]).start()
+    send_rows(0, left, sibling, fwd_send.at[0, 0]).start()
+    await_rows(0, right)
+    send_rows(0, right, sibling, fwd_send.at[0, 1]).start()
+    inner_chip(x)
+    await_rows(1, right)
+    send_rows(1, right, left, hop_send.at[1]).start()
+    send_rows(1, right, sibling, fwd_send.at[1, 1]).start()
+    await_rows(1, left)
+    send_rows(1, left, sibling, fwd_send.at[1, 0]).start()
+
+    _drain(wstep_all.at[pl.ds(0, C - 1)], step_recv)
+    states, steps = [], []
+    for h in range(2):
+        mine = rows[h, c]
+        at = slice(h * half, (h + 1) * half)
+        step_w = wstep_all[:, :, at].reshape(C * 16, half)
+        states.append(_dot(mine, w_state[at, :]))
+        steps.append(_dot(mine, step_w, ((1,), (1,))))
+    sss[...] = _fold(states[0] + states[1], steps[0] + steps[1])
+    _scatter_expert(E, sss, rss, ss_send, ss_recv)
+
+    second = 1 - lax.rem(x, 2)
+    third = jnp.where(x < 2, 2, x - 2)
+
+    def other_chip(i, carry):
+        chip = jnp.where(i == 0, second, jnp.where(i == 1, third, 6 - x - second - third))
 
         @pl.when(i == 1)
-        def _():
-            await_rows(0, left)
-            send_rows(0, left, right, hop_send.at[0]).start()
-            send_rows(0, left, sibling, fwd_send.at[0, 0]).start()
-            await_rows(0, right)
-            send_rows(0, right, sibling, fwd_send.at[0, 1]).start()
-            await_rows(1, right)
-            send_rows(1, right, left, hop_send.at[1]).start()
-            send_rows(1, right, sibling, fwd_send.at[1, 1]).start()
-            await_rows(1, left)
-            send_rows(1, left, sibling, fwd_send.at[1, 0]).start()
-
-        @pl.when(i == chips - 1)
         def _():
             for h in range(2):
                 await_rows(h, across)
                 send_rows(h, across, sibling, fwd_send.at[h, 2]).start()
-
-        for h in range(2):
-            await_rows(h, chip * 2 + 1 - core)
-        project(chip, 1, sinner)
-        _scatter_expert(E, sinner.at[chip], inner.at[chip], inner_send.at[chip], inner_recv.at[chip])
+            _drain(rss.at[peers], ss_recv)
+            vectors = rss[...].reshape(nslot, rss.shape[2])
+            at_state = _dot(_slot_onehot(row, nslot, 0), vectors, ((0,), (0,)))
+            at_step = _dot(_slot_onehot(row, nslot, 1), vectors, ((0,), (0,)))
+            ss[c] = jnp.concatenate([at_state, at_step], axis=1).astype(BF16)
+            share(ss, pos_send, pos_recv)
+
+        inner_chip(chip)
         return carry
 
-    lax.fori_loop(0, chips, inner_chip, 0)
-
-    _remote(w_out.at[c], w_out.at[c], wout_send.at[0, 0], wout_recv.at[2, c], context=sibling).start()
-    send_w_out(1, 1).start()
-    send_w_out(chips - 1, 1).start()
-
-    _drain(rss.at[peers], ss_recv)
-    here = _slot_onehot(row, nslot, 0)
-    ss[c] = _dot(here, rss[...].reshape(nslot, rss.shape[2]), ((0,), (0,))).astype(BF16)
-    share(ss, pos_send, pos_recv)
+    lax.fori_loop(0, chips - 1, other_chip, 0)
+
+    send_w_out(c, last_part, right, wout_send.at[2], 1).start()
+    send_w_out(c, last_part, left, wout_send.at[3], 1).start()
+    send_w_out(c, all_parts, sibling, wout_send.at[4], 2).start()
 
     def gate_chip(chip, carry):
         project(chip, 0, gate)
@@ -419,29 +427,18 @@
         sback[bp] = total.astype(BF16).reshape(E, 16, chans)
         _scatter_expert(E, sback.at[bp], back.at[bp], back_send.at[bp], back_recv.at[bp])
 
-        @pl.when(bp == 1)
-        def _():
-            send_w_out(2, 1).start()
-
         return carry
 
     lax.fori_loop(0, chips, pair_of_chunks, 0)
 
-    def forward_w_out(block, k):
-        pltpu.make_async_copy(
-            w_out.at[block, pl.ds(0, early)], w_out.at[block, pl.ds(0, early)], wout_recv.at[0, block]
-        ).wait()
-        rest = pl.ds(early, w_out.shape[1] - early)
-        pltpu.make_async_copy(
-            w_out.at[block, rest], w_out.at[block, rest], wout_recv.at[1, block]
-        ).wait()
-        _remote(
-            w_out.at[block], w_out.at[block], wout_send.at[1, 0] if k == 0 else fwd_send.at[k - 1, 3],
-            wout_recv.at[2, block], context=sibling,
-        ).start()
-
-    forward_w_out(right, 0)
-    forward_w_out(left, 1)
+    hops = (pl.ds(0, depth // 2), pl.ds(depth // 2, depth // 2))
+    for block in (left, right):
+        await_w_out(block, first_part, 0)
+        await_w_out(block, last_part, 1)
+    send_w_out(left, hops[0], right, wout_send.at[5], 3).start()
+    send_w_out(right, hops[1], left, wout_send.at[6], 4).start()
+    send_w_out(left, all_parts, sibling, wout_send.at[7], 2).start()
+    send_w_out(right, all_parts, sibling, wout_send.at[8], 2).start()
 
     for chip in range(chips):
         _drain(sinner.at[chip, peers], inner_send.at[chip])
@@ -450,49 +447,79 @@
         _drain(back.at[bp, peers], back_recv.at[bp])
         g = gate[bp].astype(F32)
         v = back[bp].astype(F32) * (g * jax.nn.sigmoid(g))
+        share_n = E // 4
         for part in range(2):
             mine = v[:, part * 8 : (part + 1) * 8, :].reshape(nslot // 2, chans).astype(BF16)
-            at = pl.ds(part * (E // 2), E // 2)
-            sinner[bp, at] = mine.reshape(E // 2, 16, chans)
-            target = 2 * bp + part
-
-            @pl.when(target != c)
+            sinner[bp, pl.ds(part * (E // 2), E // 2)] = mine.reshape(E // 2, 16, chans)
+
+            @pl.when(2 * bp + part == c)
             def _():
-                _remote(
-                    sinner.at[bp, at],
-                    gathered.at[c],
-                    gated_send.at[target],
-                    gated_recv.at[c],
-                    context=target,
-                ).start()
-
-            @pl.when(target == c)
-            def _():
-                gathered[c] = mine.reshape(E // 2, 16, chans)
+                gathered[c] = sinner[bp, pl.ds(part * (E // 2), E // 2)]
+
+        for group in range(2):
+            for part in range(2):
+                target = 2 * bp + part
+
+                @pl.when(target != c)
+                def _():
+                    _remote(
+                        sinner.at[bp, pl.ds((part * 2 + group) * share_n, share_n)],
+                        gathered.at[c, pl.ds(group * share_n, share_n)],
+                        gated_send.at[group, target],
+                        gated_recv.at[group, c],
+                        context=target,
+                    ).start()
+
+        @pl.when(bp == chips - 2)
+        def _():
+            await_w_out(across, hops[0], 3)
+            await_w_out(across, hops[1], 4)
+            send_w_out(across, all_parts, sibling, wout_send.at[9], 2).start()
 
         return carry
 
     lax.fori_loop(0, chips, gate_rows, 0)
-    forward_w_out(across, 2)
-
-    for k in range(1, C):
-        block = lax.rem(c + k, C)
-        _drain(gathered.at[block], gated_recv.at[block])
+
     for k in range(chips):
-        block = lax.rem(x + k, chips) * 2 + 1 - core
-        _drain(w_out.at[block], wout_recv.at[2, block])
+        await_w_out(lax.rem(x + k, chips) * 2 + 1 - core, all_parts, 2)
     parts, _, _, fin_n = fin_src.shape
-
-    def finish(j, carry):
-        total = jnp.zeros((nrow, 2 * fin_n), F32)
-        cols = pl.ds(pl.multiple_of(j * 2 * fin_n, 2 * fin_n), 2 * fin_n)
-        for block in range(C):
-            total = total + _dot(gathered[block].reshape(nrow, chans), w_out[block, :, cols])
-        fin_src[j] = _fold(total[:, :fin_n], total[:, fin_n:])
-        _scatter_expert(E, fin_src.at[j], fin_dst.at[j], fin_send.at[j], fin_recv.at[j])
+    seqs, share_n = E // 2, E // 4
+
+    def finish(group, carry):
+        for k in range(1, C):
+            block = lax.rem(c + k, C)
+            _drain(gathered.at[block, pl.ds(0, share_n)], gated_recv.at[group, block])
+
+        def columns_of(j, carry):
+            total = jnp.zeros((nrow // 2, 2 * fin_n), F32)
+            cols = pl.ds(pl.multiple_of(j * 2 * fin_n, 2 * fin_n), 2 * fin_n)
+            for block in range(C):
+                mine = gathered[block, pl.ds(group * share_n, share_n)].reshape(nrow // 2, chans)
+                total = total + _dot(mine, w_out[block, :, cols])
+            fin_src[j, pl.ds(group * seqs, seqs)] = _fold(total[:, :fin_n], total[:, fin_n:])
+
+            def send(k, carry):
+                peer = group * seqs + lax.rem(e + k, seqs)
+
+                @pl.when(peer != e)
+                def _():
+                    _remote(
+                        fin_src.at[j, peer], fin_dst.at[j, e], fin_send.at[j], fin_recv.at[j], expert=peer
+                    ).start()
+
+                @pl.when(peer == e)
+                def _():
+                    fin_dst[j, e] = fin_src[j, e]
+
+                return carry
+
+            lax.fori_loop(0, seqs, send, 0)
+            return carry
+
+        lax.fori_loop(0, parts, columns_of, 0)
         return carry
 
-    lax.fori_loop(0, parts, finish, 0)
+    lax.fori_loop(0, 2, finish, 0)
 
     places = [_slot_onehot(row, nslot, part) for part in range(2)]
     for j in range(parts):
@@ -515,16 +542,12 @@
         _drain(sback.at[chip, peers], back_send.at[chip])
     for k in range(1, C):
         target = lax.rem(c + k, C)
-        _drain(gathered.at[0], gated_send.at[target])
+        for group in range(2):
+            _drain(gathered.at[0, pl.ds(0, share_n)], gated_send.at[group, target])
     for j in range(parts):
         _drain(fin_src.at[j, peers], fin_send.at[j])
-    for k in range(1, chips):
-        _drain(w_out.at[0, pl.ds(0, early)], wout_send.at[0, k])
-        _drain(w_out.at[0, pl.ds(early, w_out.shape[1] - early)], wout_send.at[1, k])
-    _drain(w_out.at[0], wout_send.at[0, 0])
-    _drain(w_out.at[0], wout_send.at[1, 0])
-    _drain(w_out.at[0], fwd_send.at[0, 3])
-    _drain(w_out.at[0], fwd_send.at[1, 3])
+    for k, where in enumerate((first_part, first_part, last_part, last_part, all_parts) + hops + (all_parts,) * 3):
+        _drain(w_out.at[0, where], wout_send.at[k])
 
 
 def per_device(
@@ -570,8 +593,8 @@
             flat,
             flat,
             pltpu.VMEM((C, 16, width), BF16),
-            pltpu.VMEM((E, 16, wide), BF16),
-            pltpu.VMEM((E, 16, wide), BF16),
+            pltpu.VMEM((E, 16, wide // 2), BF16),
+            pltpu.VMEM((E, 16, wide // 2), BF16),
             pltpu.VMEM((C, T, wide), BF16),
             pltpu.VMEM((C, E // 2, 16, chans), BF16),
             pltpu.VMEM((parts, E, 16, fin_n), BF16),
@@ -587,7 +610,7 @@
             dma,
             dma((2, 3)),
             dma((2, C)),
-            dma((2, 4)),
+            dma((2, 3)),
             dma((2,)),
             dma,
             dma,
@@ -595,12 +618,12 @@
             dma,
             dma((chips,)),
             dma((chips,)),
-            dma((2, chips)),
-            dma((3, C)),
+            dma((10,)),
+            dma((5, C)),
             dma((chips,)),
             dma((chips,)),
-            dma((C,)),
-            dma((C,)),
+            dma((2, C)),
+            dma((2, C)),
             dma((parts,)),
             dma((parts,)),
         ],

time: 220 us -> 191 us (0.87)
  the two profiles are of different devices: /device:TPU:7 before, /device:TPU:23 now
where the time goes in v3:
time: 191 us; the launch traced here: 190 us
  Pallas kernels  189 us (99%)
    pallas_call x1, Pallas kernels, per_device(): pl.pallas_call(functools.partial(layer_kernel, E, C), out_shape=jax.Shape...  189 us

profile of v3, /device:TPU:23, one launch (start us, length us, event | category | flops | bytes accessed | tf_op | source)
XLA Modules:
  0.0 190.4 jit_solution(583594579385451638)
XLA Ops:
  0.0 188.5 %layer.1 = bf16[128,2048]{1,0:T(8,128)(2,1)} custom-call(s32[8,128]{1,0:T(8,128)} %bitcast.19, bf16[128,2048]{1,0:T(8,128)(2,1)} %bitcast.16, bf16[2048,2,512]{2,1,0:T(2,128)(2,1)} %bitcast.13, bf16[2048,128]{1,0:T(8,128)(2,1)} %bitcast.17, bf16[8,2048]{1,0:T(8,128)(2,1)} %bitcast.18, f32[1,8]{1,0:T(1,128)} %bitcast.21, f32[1,8]{1,0:T(1,128)} %bitcast.22, ...), custom_call_target="tpu_custom_call" | custom-call | tf_op jit(solution)/shard_map/layer/pallas_call | solution.py:577
  188.6 1.9 copy.13

commit v4 on v3

--- a/solution.py
+++ b/solution.py
@@ -32,10 +32,24 @@
 
     greet("expert", e, expert_peers)
     greet("context", c, context_peers)
+    owner = e // (expert_peers // context_peers)
+
+    def greet_owner(k, carry):
+        @pl.when((k != e) | (owner != c))
+        def _():
+            pl.semaphore_signal(
+                barrier, inc=1, device_id={"expert": k, "context": owner}, device_id_type=MESH
+            )
+
+        return carry
+
+    lax.fori_loop(0, expert_peers, greet_owner, 0)
 
 
 def _meet(expert_peers, context_peers):
-    pl.semaphore_wait(pltpu.get_barrier_semaphore(), expert_peers + context_peers - 2)
+    e, c = lax.axis_index("expert"), lax.axis_index("context")
+    own = jnp.where(e // (expert_peers // context_peers) == c, 1, 0)
+    pl.semaphore_wait(pltpu.get_barrier_semaphore(), 2 * expert_peers + context_peers - 2 - own)
 
 
 def _drain(ref, sem):
@@ -154,6 +168,7 @@
     inner_recv,
     wout_send,
     wout_recv,
+    across_send,
     back_send,
     back_recv,
     gated_send,
@@ -175,7 +190,7 @@
     pieces, piece = w3.shape[0], w3.shape[1]
     count = width // piece
     depth = w_out.shape[1]
-    early = depth // 16 * 5
+    early = depth // 16 * 4
     peers = pl.ds(0, E - 1)
 
     def load_piece(q):
@@ -238,7 +253,9 @@
     def await_w_out(block, where, kind):
         _drain(w_out.at[block, where], wout_recv.at[kind, block])
 
-    first_part, last_part, all_parts = pl.ds(0, early), pl.ds(early, depth - early), pl.ds(0, depth)
+    first_part, next_part = pl.ds(0, early), pl.ds(early, depth // 2 - early)
+    last_part, all_parts = pl.ds(depth // 2, depth // 2), pl.ds(0, depth)
+    hops = (pl.ds(0, depth // 2), last_part)
     load_w_out.wait()
     send_w_out(c, first_part, right, wout_send.at[0], 0).start()
     send_w_out(c, first_part, left, wout_send.at[1], 0).start()
@@ -271,34 +288,6 @@
         send_rows(h, c, right, row_send.at[h, 0]).start()
         send_rows(h, c, left, row_send.at[h, 1]).start()
         send_rows(h, c, sibling, row_send.at[h, 2]).start()
-
-    step_n = min(256, chans)
-
-    def project(chip, which, dst):
-        first = rows[0, pl.ds(chip * 2, 2)].reshape(2 * nrow, half)
-        second = rows[1, pl.ds(chip * 2, 2)].reshape(2 * nrow, half)
-        for n in range(chans // step_n):
-            cols = slice(n * step_n, (n + 1) * step_n)
-            res = _dot(first, w_inner[which, :half, cols]) + _dot(second, w_inner[which, half:, cols])
-            dst[chip, :, :, cols] = _fold(res[:nrow], res[nrow:])
-
-    def inner_chip(chip):
-        for h in range(2):
-            await_rows(h, chip * 2 + 1 - core)
-        project(chip, 1, sinner)
-        _scatter_expert(E, sinner.at[chip], inner.at[chip], inner_send.at[chip], inner_recv.at[chip])
-
-    await_rows(0, left)
-    send_rows(0, left, right, hop_send.at[0]).start()
-    send_rows(0, left, sibling, fwd_send.at[0, 0]).start()
-    await_rows(0, right)
-    send_rows(0, right, sibling, fwd_send.at[0, 1]).start()
-    inner_chip(x)
-    await_rows(1, right)
-    send_rows(1, right, left, hop_send.at[1]).start()
-    send_rows(1, right, sibling, fwd_send.at[1, 1]).start()
-    await_rows(1, left)
-    send_rows(1, left, sibling, fwd_send.at[1, 0]).start()
 
     _drain(wstep_all.at[pl.ds(0, C - 1)], step_recv)
     states, steps = [], []
@@ -311,6 +300,47 @@
     sss[...] = _fold(states[0] + states[1], steps[0] + steps[1])
     _scatter_expert(E, sss, rss, ss_send, ss_recv)
 
+    step_n = min(256, chans)
+
+    def project(chip, which, dst):
+        first = rows[0, pl.ds(chip * 2, 2)].reshape(2 * nrow, half)
+        second = rows[1, pl.ds(chip * 2, 2)].reshape(2 * nrow, half)
+        for n in range(chans // step_n):
+            cols = slice(n * step_n, (n + 1) * step_n)
+            res = _dot(first, w_inner[which, :half, cols]) + _dot(second, w_inner[which, half:, cols])
+            dst[chip, :, :, cols] = _fold(res[:nrow], res[nrow:])
+
+    def inner_chip(chip):
+        for h in range(2):
+            await_rows(h, chip * 2 + 1 - core)
+        project(chip, 1, sinner)
+        _scatter_expert(E, sinner.at[chip], inner.at[chip], inner_send.at[chip], inner_recv.at[chip])
+
+    inner_chip(x)
+    await_rows(0, left)
+    send_rows(0, left, right, hop_send.at[0]).start()
+    send_rows(0, left, sibling, fwd_send.at[0, 0]).start()
+    await_rows(0, right)
+    send_rows(0, right, sibling, fwd_send.at[0, 1]).start()
+    await_rows(1, right)
+    send_rows(1, right, left, hop_send.at[1]).start()
+    send_rows(1, right, sibling, fwd_send.at[1, 1]).start()
+    await_rows(1, left)
+    send_rows(1, left, sibling, fwd_send.at[1, 0]).start()
+
+    _drain(rss.at[peers], ss_recv)
+    vectors = rss[...].reshape(nslot, rss.shape[2])
+    at_state = _dot(_slot_onehot(row, nslot, 0), vectors, ((0,), (0,)))
+    at_step = _dot(_slot_onehot(row, nslot, 1), vectors, ((0,), (0,)))
+    ss[c] = jnp.concatenate([at_state, at_step], axis=1).astype(BF16)
+    share(ss, pos_send, pos_recv)
+
+    send_w_out(c, next_part, right, wout_send.at[9], 5).start()
+    send_w_out(c, last_part, left, wout_send.at[3], 1).start()
+    send_w_out(c, last_part, right, wout_send.at[2], 1).start()
+    send_w_out(c, next_part, left, wout_send.at[10], 5).start()
+    send_w_out(c, all_parts, sibling, wout_send.at[4], 2).start()
+
     second = 1 - lax.rem(x, 2)
     third = jnp.where(x < 2, 2, x - 2)
 
@@ -322,21 +352,11 @@
             for h in range(2):
                 await_rows(h, across)
                 send_rows(h, across, sibling, fwd_send.at[h, 2]).start()
-            _drain(rss.at[peers], ss_recv)
-            vectors = rss[...].reshape(nslot, rss.shape[2])
-            at_state = _dot(_slot_onehot(row, nslot, 0), vectors, ((0,), (0,)))
-            at_step = _dot(_slot_onehot(row, nslot, 1), vectors, ((0,), (0,)))
-            ss[c] = jnp.concatenate([at_state, at_step], axis=1).astype(BF16)
-            share(ss, pos_send, pos_recv)
 
         inner_chip(chip)
         return carry
 
     lax.fori_loop(0, chips - 1, other_chip, 0)
-
-    send_w_out(c, last_part, right, wout_send.at[2], 1).start()
-    send_w_out(c, last_part, left, wout_send.at[3], 1).start()
-    send_w_out(c, all_parts, sibling, wout_send.at[4], 2).start()
 
     def gate_chip(chip, carry):
         project(chip, 0, gate)
@@ -417,6 +437,15 @@
 
     def pair_of_chunks(bp, carry):
         _drain(inner.at[bp, peers], inner_recv.at[bp])
+
+        @pl.when(bp == chips - 1)
+        def _():
+            await_w_out(left, first_part, 0)
+            await_w_out(left, next_part, 5)
+            send_w_out(left, hops[0], right, wout_send.at[5], 3).start()
+            await_w_out(right, last_part, 1)
+            send_w_out(right, hops[1], left, wout_send.at[6], 4).start()
+
         chunk(2 * bp, 0)
         chunk(2 * bp + 1, 1)
         total = None
@@ -431,103 +460,117 @@
 
     lax.fori_loop(0, chips, pair_of_chunks, 0)
 
-    hops = (pl.ds(0, depth // 2), pl.ds(depth // 2, depth // 2))
-    for block in (left, right):
-        await_w_out(block, first_part, 0)
-        await_w_out(block, last_part, 1)
-    send_w_out(left, hops[0], right, wout_send.at[5], 3).start()
-    send_w_out(right, hops[1], left, wout_send.at[6], 4).start()
-    send_w_out(left, all_parts, sibling, wout_send.at[7], 2).start()
-    send_w_out(right, all_parts, sibling, wout_send.at[8], 2).start()
-
     for chip in range(chips):
         _drain(sinner.at[chip, peers], inner_send.at[chip])
+
+    group = E // C
 
     def gate_rows(bp, carry):
         _drain(back.at[bp, peers], back_recv.at[bp])
         g = gate[bp].astype(F32)
         v = back[bp].astype(F32) * (g * jax.nn.sigmoid(g))
-        share_n = E // 4
+        sinner[bp] = v.astype(BF16)
+
+        def send(k, carry):
+            target = lax.rem(c + k, C)
+            _remote(
+                sinner.at[bp, pl.ds(target * group, group)],
+                gathered.at[bp, c],
+                gated_send.at[bp],
+                gated_recv.at[bp],
+                context=target,
+            ).start()
+            return carry
+
+        lax.fori_loop(1, C, send, 0)
+        gathered[bp, c] = sinner[bp, pl.ds(c * group, group)]
+        return carry
+
+    half_n = half // 2
+
+    def multiply(bp, carry):
+        _drain(gathered.at[bp, pl.ds(0, C - 1)], gated_recv.at[bp])
+
+        def columns_of(j, carry):
+            sums = []
+            for late in range(2):
+                total = jnp.zeros((group * 16, half_n), F32)
+                cols = pl.ds(pl.multiple_of(late * half + j * half_n, half_n), half_n)
+                for block in range(C):
+                    mine = gathered[bp, block].reshape(group * 16, chans)
+                    total = total + _dot(mine, w_out[block, :, cols])
+                sums.append(total)
+            fin_src[bp, :, :, pl.ds(pl.multiple_of(j * half_n, half_n), half_n)] = _fold(*sums)
+            return carry
+
+        lax.fori_loop(0, 2, columns_of, 0)
+        return carry
+
+    def send_final(bp, carry):
+        def send(q, carry):
+            seq, block = c * group + q // 2, 2 * bp + lax.rem(q, 2)
+            here = (seq == e) & (block == c)
+
+            @pl.when(jnp.logical_not(here))
+            def _():
+                _remote(
+                    fin_src.at[bp, q],
+                    fin_dst.at[e],
+                    fin_send.at[bp * 2 * group + q],
+                    fin_recv.at[e],
+                    expert=seq,
+                    context=block,
+                ).start()
+
+            @pl.when(here)
+            def _():
+                fin_dst[e] = fin_src[bp, q]
+
+            return carry
+
+        lax.fori_loop(0, 2 * group, send, 0)
+        return carry
+
+    await_w_out(right, first_part, 0)
+    await_w_out(right, next_part, 5)
+    send_w_out(right, all_parts, sibling, wout_send.at[8], 2).start()
+    await_w_out(left, last_part, 1)
+    send_w_out(left, all_parts, sibling, wout_send.at[7], 2).start()
+    lax.fori_loop(0, chips - 1, gate_rows, 0)
+    for k in range(2):
+        await_w_out(across, hops[k], 3 + k)
+        send_w_out(across, hops[k], sibling, across_send.at[k], 3 + k).start()
+    gate_rows(chips - 1, 0)
+    for block in (sibling, left + 1 - 2 * core, right + 1 - 2 * core):
+        await_w_out(block, all_parts, 2)
+    for k in range(2):
+        await_w_out(across + 1 - 2 * core, hops[k], 3 + k)
+    lax.fori_loop(0, chips - 2, multiply, 0)
+    lax.fori_loop(0, chips - 2, send_final, 0)
+
+    def last_blocks(bp, carry):
+        multiply(bp, 0)
+        send_final(bp, 0)
+        return carry
+
+    lax.fori_loop(chips - 2, chips, last_blocks, 0)
+
+    places = [_slot_onehot(row, nslot, part) for part in range(2)]
+    at_owner = c == e // group
+
+    def await_final(k, carry):
+        @pl.when(jnp.logical_not((k == e) & at_owner))
+        def _():
+            _drain(fin_dst.at[k], fin_recv.at[k])
+
+        return carry
+
+    lax.fori_loop(0, E, await_final, 0)
+    for j in range(2):
+        arrived = fin_dst[:, :, j * half_n : (j + 1) * half_n].reshape(nslot, half_n)
         for part in range(2):
-            mine = v[:, part * 8 : (part + 1) * 8, :].reshape(nslot // 2, chans).astype(BF16)
-            sinner[bp, pl.ds(part * (E // 2), E // 2)] = mine.reshape(E // 2, 16, chans)
-
-            @pl.when(2 * bp + part == c)
-            def _():
-                gathered[c] = sinner[bp, pl.ds(part * (E // 2), E // 2)]
-
-        for group in range(2):
-            for part in range(2):
-                target = 2 * bp + part
-
-                @pl.when(target != c)
-                def _():
-                    _remote(
-                        sinner.at[bp, pl.ds((part * 2 + group) * share_n, share_n)],
-                        gathered.at[c, pl.ds(group * share_n, share_n)],
-                        gated_send.at[group, target],
-                        gated_recv.at[group, c],
-                        context=target,
-                    ).start()
-
-        @pl.when(bp == chips - 2)
-        def _():
-            await_w_out(across, hops[0], 3)
-            await_w_out(across, hops[1], 4)
-            send_w_out(across, all_parts, sibling, wout_send.at[9], 2).start()
-
-        return carry
-
-    lax.fori_loop(0, chips, gate_rows, 0)
-
-    for k in range(chips):
-        await_w_out(lax.rem(x + k, chips) * 2 + 1 - core, all_parts, 2)
-    parts, _, _, fin_n = fin_src.shape
-    seqs, share_n = E // 2, E // 4
-
-    def finish(group, carry):
-        for k in range(1, C):
-            block = lax.rem(c + k, C)
-            _drain(gathered.at[block, pl.ds(0, share_n)], gated_recv.at[group, block])
-
-        def columns_of(j, carry):
-            total = jnp.zeros((nrow // 2, 2 * fin_n), F32)
-            cols = pl.ds(pl.multiple_of(j * 2 * fin_n, 2 * fin_n), 2 * fin_n)
-            for block in range(C):
-                mine = gathered[block, pl.ds(group * share_n, share_n)].reshape(nrow // 2, chans)
-                total = total + _dot(mine, w_out[block, :, cols])
-            fin_src[j, pl.ds(group * seqs, seqs)] = _fold(total[:, :fin_n], total[:, fin_n:])
-
-            def send(k, carry):
-                peer = group * seqs + lax.rem(e + k, seqs)
-
-                @pl.when(peer != e)
-                def _():
-                    _remote(
-                        fin_src.at[j, peer], fin_dst.at[j, e], fin_send.at[j], fin_recv.at[j], expert=peer
-                    ).start()
-
-                @pl.when(peer == e)
-                def _():
-                    fin_dst[j, e] = fin_src[j, e]
-
-                return carry
-
-            lax.fori_loop(0, seqs, send, 0)
-            return carry
-
-        lax.fori_loop(0, parts, columns_of, 0)
-        return carry
-
-    lax.fori_loop(0, 2, finish, 0)
-
-    places = [_slot_onehot(row, nslot, part) for part in range(2)]
-    for j in range(parts):
-        _drain(fin_dst.at[j, peers], fin_recv.at[j])
-        arrived = fin_dst[j].reshape(nslot, fin_n)
-        for part in range(2):
-            begin = (2 * j + part) * fin_n
-            out[:, begin : begin + fin_n] = _dot(places[part], arrived, ((0,), (0,))).astype(BF16)
+            begin = part * half + j * half_n
+            out[:, begin : begin + half_n] = _dot(places[part], arrived, ((0,), (0,))).astype(BF16)
 
     for h in range(2):
         _drain(stok.at[h, peers], tok_send.at[h])
@@ -540,14 +583,23 @@
     _drain(ss.at[pl.ds(0, C - 1)], pos_send)
     for chip in range(chips):
         _drain(sback.at[chip, peers], back_send.at[chip])
-    for k in range(1, C):
-        target = lax.rem(c + k, C)
-        for group in range(2):
-            _drain(gathered.at[0, pl.ds(0, share_n)], gated_send.at[group, target])
-    for j in range(parts):
-        _drain(fin_src.at[j, peers], fin_send.at[j])
-    for k, where in enumerate((first_part, first_part, last_part, last_part, all_parts) + hops + (all_parts,) * 3):
+    for bp in range(chips):
+        _drain(gathered.at[bp, pl.ds(0, C - 1)], gated_send.at[bp])
+
+    def left_final(k, carry):
+        bp, q = k // (2 * group), lax.rem(k, 2 * group)
+
+        @pl.when(jnp.logical_not((c * group + q // 2 == e) & (2 * bp + lax.rem(q, 2) == c)))
+        def _():
+            _drain(fin_src.at[bp, q], fin_send.at[k])
+
+        return carry
+
+    lax.fori_loop(0, E, left_final, 0)
+    for k, where in enumerate((first_part, first_part, last_part, last_part, all_parts) + hops + (all_parts,) * 2 + (next_part,) * 2):
         _drain(w_out.at[0, where], wout_send.at[k])
+    for k in range(2):
+        _drain(w_out.at[0, hops[k]], across_send.at[k])
 
 
 def per_device(
@@ -568,8 +620,6 @@
     chips = C // 2
     chans = w_inner.shape[3]
     wide = w_state.shape[2] + C * 16
-    parts = 4
-    fin_n = width // parts // 2
     vmem = pl.BlockSpec(memory_space=pltpu.VMEM)
     hbm = pl.BlockSpec(memory_space=pl.ANY)
     dma = pltpu.SemaphoreType.DMA
@@ -596,9 +646,9 @@
             pltpu.VMEM((E, 16, wide // 2), BF16),
             pltpu.VMEM((E, 16, wide // 2), BF16),
             pltpu.VMEM((C, T, wide), BF16),
-            pltpu.VMEM((C, E // 2, 16, chans), BF16),
-            pltpu.VMEM((parts, E, 16, fin_n), BF16),
-            pltpu.VMEM((parts, E, 16, fin_n), BF16),
+            pltpu.VMEM((chips, C, E // C, 16, chans), BF16),
+            pltpu.VMEM((chips, 2 * (E // C), 16, width // 2), BF16),
+            pltpu.VMEM((E, 16, width // 2), BF16),
             pltpu.VMEM((HEAD_DIM, chans), F32),
             pltpu.VMEM((8, chans), F32),
             pltpu.VMEM((2, T, chans), BF16),
@@ -618,14 +668,15 @@
             dma,
             dma((chips,)),
             dma((chips,)),
-            dma((10,)),
-            dma((5, C)),
+            dma((11,)),
+            dma((6, C)),
+            dma((2,)),
             dma((chips,)),
             dma((chips,)),
-            dma((2, C)),
-            dma((2, C)),
-            dma((parts,)),
-            dma((parts,)),
+            dma((chips,)),
+            dma((chips,)),
+            dma((E,)),
+            dma((E,)),
         ],
         compiler_params=pltpu.CompilerParams(
             collective_id=0, has_side_effects=True, vmem_limit_bytes=VMEM_LIMIT

time: 191 us -> 183 us (0.958)
  the two profiles are of different devices: /device:TPU:23 before, /device:TPU:7 now
where the time goes in v4:
time: 183 us; the launch traced here: 180 us
  Pallas kernels  178 us (97%)
  local copies, waits for them, and re-layouts  1.88 us (1%)
    pallas_call x1, Pallas kernels, per_device(): pl.pallas_call(functools.partial(layer_kernel, E, C), out_shape=jax.Shape...  178 us

profile of v4, /device:TPU:7, one launch (start us, length us, event | category | flops | bytes accessed | tf_op | source)
XLA Modules:
  0.0 180.2 jit_solution(4492169392925068015)
XLA Ops:
  0.0 178.3 %layer.1 = bf16[128,2048]{1,0:T(8,128)(2,1)} custom-call(s32[8,128]{1,0:T(8,128)} %bitcast.19, bf16[128,2048]{1,0:T(8,128)(2,1)} %bitcast.16, bf16[2048,2,512]{2,1,0:T(2,128)(2,1)} %bitcast.13, bf16[2048,128]{1,0:T(8,128)(2,1)} %bitcast.17, bf16[8,2048]{1,0:T(8,128)(2,1)} %bitcast.18, f32[1,8]{1,0:T(1,128)} %bitcast.21, f32[1,8]{1,0:T(1,128)} %bitcast.22, ...), custom_call_target="tpu_custom_call" | custom-call | tf_op jit(solution)/shard_map/layer/pallas_call | solution.py:627
  178.3 1.9 %copy.13 = bf16[1,128,2048]{2,1,0:T(8,128)(2,1)} copy(bf16[1,128,2048]{2,1,0:T(8,128)(2,1)} %bitcast.15) | data formatting | bytes 1048576

commit v5 on v4

--- a/solution.py
+++ b/solution.py
@@ -18,6 +18,10 @@
     return lax.dot_general(a, b, (dims, ((), ())), precision=precision, preferred_element_type=F32)
 
 
+def _owner(seq, expert, E, C):
+    return lax.rem(seq // (E // C) + expert, C)
+
+
 def _greet(expert_peers, context_peers):
     e, c = lax.axis_index("expert"), lax.axis_index("context")
     barrier = pltpu.get_barrier_semaphore()
@@ -32,9 +36,10 @@
 
     greet("expert", e, expert_peers)
     greet("context", c, context_peers)
-    owner = e // (expert_peers // context_peers)
 
     def greet_owner(k, carry):
+        owner = _owner(e, k, expert_peers, context_peers)
+
         @pl.when((k != e) | (owner != c))
         def _():
             pl.semaphore_signal(
@@ -48,7 +53,7 @@
 
 def _meet(expert_peers, context_peers):
     e, c = lax.axis_index("expert"), lax.axis_index("context")
-    own = jnp.where(e // (expert_peers // context_peers) == c, 1, 0)
+    own = jnp.where(_owner(e, e, expert_peers, context_peers) == c, 1, 0)
     pl.semaphore_wait(pltpu.get_barrier_semaphore(), 2 * expert_peers + context_peers - 2 - own)
 
 
@@ -465,6 +470,9 @@
 
     group = E // C
 
+    def first_of(owner):
+        return lax.rem(owner + C - lax.rem(e, C), C) * group
+
     def gate_rows(bp, carry):
         _drain(back.at[bp, peers], back_recv.at[bp])
         g = gate[bp].astype(F32)
@@ -474,7 +482,7 @@
         def send(k, carry):
             target = lax.rem(c + k, C)
             _remote(
-                sinner.at[bp, pl.ds(target * group, group)],
+                sinner.at[bp, pl.ds(first_of(target), group)],
                 gathered.at[bp, c],
                 gated_send.at[bp],
                 gated_recv.at[bp],
@@ -483,32 +491,36 @@
             return carry
 
         lax.fori_loop(1, C, send, 0)
-        gathered[bp, c] = sinner[bp, pl.ds(c * group, group)]
+        gathered[bp, c] = sinner[bp, pl.ds(first_of(c), group)]
         return carry
 
     half_n = half // 2
 
-    def multiply(bp, carry):
-        _drain(gathered.at[bp, pl.ds(0, C - 1)], gated_recv.at[bp])
+    def multiply(begin, end):
+        for bp in range(begin, end):
+            _drain(gathered.at[bp, pl.ds(0, C - 1)], gated_recv.at[bp])
+        count_rows = (end - begin) * group * 16
 
         def columns_of(j, carry):
             sums = []
             for late in range(2):
-                total = jnp.zeros((group * 16, half_n), F32)
+                total = jnp.zeros((count_rows, half_n), F32)
                 cols = pl.ds(pl.multiple_of(late * half + j * half_n, half_n), half_n)
                 for block in range(C):
-                    mine = gathered[bp, block].reshape(group * 16, chans)
+                    mine = gathered[begin:end, block].reshape(count_rows, chans)
                     total = total + _dot(mine, w_out[block, :, cols])
                 sums.append(total)
-            fin_src[bp, :, :, pl.ds(pl.multiple_of(j * half_n, half_n), half_n)] = _fold(*sums)
+            at = pl.ds(pl.multiple_of(j * half_n, half_n), half_n)
+            folded = _fold(*sums).reshape(end - begin, 2 * group, 16, half_n)
+            fin_src[begin:end, :, :, at] = folded
             return carry
 
         lax.fori_loop(0, 2, columns_of, 0)
-        return carry
-
-    def send_final(bp, carry):
-        def send(q, carry):
-            seq, block = c * group + q // 2, 2 * bp + lax.rem(q, 2)
+
+    def send_final(begin, end):
+        def send(k, carry):
+            q, bp = k // (end - begin), begin + lax.rem(k + x, end - begin)
+            seq, block = first_of(c) + q // 2, 2 * bp + lax.rem(q, 2)
             here = (seq == e) & (block == c)
 
             @pl.when(jnp.logical_not(here))
@@ -528,8 +540,7 @@
 
             return carry
 
-        lax.fori_loop(0, 2 * group, send, 0)
-        return carry
+        lax.fori_loop(0, (end - begin) * 2 * group, send, 0)
 
     await_w_out(right, first_part, 0)
     await_w_out(right, next_part, 5)
@@ -545,18 +556,16 @@
         await_w_out(block, all_parts, 2)
     for k in range(2):
         await_w_out(across + 1 - 2 * core, hops[k], 3 + k)
-    lax.fori_loop(0, chips - 2, multiply, 0)
-    lax.fori_loop(0, chips - 2, send_final, 0)
-
-    def last_blocks(bp, carry):
-        multiply(bp, 0)
-        send_final(bp, 0)
-        return carry
-
-    lax.fori_loop(chips - 2, chips, last_blocks, 0)
-
-    places = [_slot_onehot(row, nslot, part) for part in range(2)]
-    at_owner = c == e // group
+    multiply(0, chips // 2)
+    send_final(0, chips // 2)
+    for bp in range(chips // 2, chips):
+        multiply(bp, bp + 1)
+        send_final(bp, bp + 1)
+
+    places = [
+        _dot(eye, _slot_onehot(row, nslot, part), ((1,), (1,))).astype(BF16) for part in range(2)
+    ]
+    at_owner = c == _owner(e, e, E, C)
 
     def await_final(k, carry):
         @pl.when(jnp.logical_not((k == e) & at_owner))
@@ -570,7 +579,7 @@
         arrived = fin_dst[:, :, j * half_n : (j + 1) * half_n].reshape(nslot, half_n)
         for part in range(2):
             begin = part * half + j * half_n
-            out[:, begin : begin + half_n] = _dot(places[part], arrived, ((0,), (0,))).astype(BF16)
+            out[:, begin : begin + half_n] = _dot(places[part], arrived).astype(BF16)
 
     for h in range(2):
         _drain(stok.at[h, peers], tok_send.at[h])
@@ -589,7 +598,7 @@
     def left_final(k, carry):
         bp, q = k // (2 * group), lax.rem(k, 2 * group)
 
-        @pl.when(jnp.logical_not((c * group + q // 2 == e) & (2 * bp + lax.rem(q, 2) == c)))
+        @pl.when(jnp.logical_not((first_of(c) + q // 2 == e) & (2 * bp + lax.rem(q, 2) == c)))
         def _():
             _drain(fin_src.at[bp, q], fin_send.at[k])
 

time: 183 us -> 180 us (0.984); the launches traced: 180 us -> 180 us
  no operation moved by 1% of the time
where the time goes in v5:
time: 180 us
  Pallas kernels  178 us (99%)
  local copies, waits for them, and re-layouts  1.88 us (1%)
    pallas_call x1, Pallas kernels, per_device(): pl.pallas_call(functools.partial(layer_kernel, E, C), out_shape=jax.Shape...  178 us

profile of v5, /device:TPU:7, one launch (start us, length us, event | category | flops | bytes accessed | tf_op | source)
XLA Modules:
  0.0 180.3 jit_solution(13309368469417807234)
XLA Ops:
  0.0 178.4 %layer.1 = bf16[128,2048]{1,0:T(8,128)(2,1)} custom-call(s32[8,128]{1,0:T(8,128)} %bitcast.19, bf16[128,2048]{1,0:T(8,128)(2,1)} %bitcast.16, bf16[2048,2,512]{2,1,0:T(2,128)(2,1)} %bitcast.13, bf16[2048,128]{1,0:T(8,128)(2,1)} %bitcast.17, bf16[8,2048]{1,0:T(8,128)(2,1)} %bitcast.18, f32[1,8]{1,0:T(1,128)} %bitcast.21, f32[1,8]{1,0:T(1,128)} %bitcast.22, ...), custom_call_target="tpu_custom_call" | custom-call | tf_op jit(solution)/shard_map/layer/pallas_call | solution.py:636
  178.4 1.9 %copy.13 = bf16[1,128,2048]{2,1,0:T(8,128)(2,1)} copy(bf16[1,128,2048]{2,1,0:T(8,128)(2,1)} %bitcast.15) | data formatting | bytes 1048576

commit v6 on v5

--- a/solution.py
+++ b/solution.py
@@ -122,9 +122,9 @@
     E,
     C,
     ids,
-    tokens,
+    tokens_hbm,
     w_inner_hbm,
-    w_state,
+    w_state_hbm,
     w_step,
     step_bias,
     decay_log,
@@ -133,6 +133,8 @@
     conv_bias,
     w_out_hbm,
     out,
+    tokens,
+    w_state,
     slots,
     w3,
     w_inner,
@@ -155,6 +157,7 @@
     state,
     tail8,
     scanned,
+    in_sem,
     w3_sem,
     w_sem,
     tok_send,
@@ -204,6 +207,10 @@
         )
 
     _greet(E, C)
+    load_tokens = pltpu.make_async_copy(tokens_hbm, tokens, in_sem.at[0])
+    load_tokens.start()
+    load_w_state = pltpu.make_async_copy(w_state_hbm, w_state, in_sem.at[1])
+    load_w_state.start()
     for q in range(pieces):
         load_piece(q).start()
     load_w_out = pltpu.make_async_copy(w_out_hbm, w_out.at[c], w_sem)
@@ -228,6 +235,7 @@
             _dot(dispatch, tokens[:, a + quarter : a + half]),
         )
 
+    load_tokens.wait()
     pack(0)
     _meet(E, C)
     _scatter_expert(E, stok.at[0], rtok.at[0], tok_send.at[0], tok_recv.at[0])
@@ -295,6 +303,7 @@
         send_rows(h, c, sibling, row_send.at[h, 2]).start()
 
     _drain(wstep_all.at[pl.ds(0, C - 1)], step_recv)
+    load_w_state.wait()
     states, steps = [], []
     for h in range(2):
         mine = rows[h, c]
@@ -636,9 +645,11 @@
     mixed = pl.pallas_call(
         functools.partial(layer_kernel, E, C),
         out_shape=jax.ShapeDtypeStruct((T, width), BF16),
-        in_specs=[vmem, vmem, hbm, vmem, vmem, vmem, vmem, vmem, vmem, vmem, hbm],
+        in_specs=[vmem, hbm, hbm, hbm, vmem, vmem, vmem, vmem, vmem, vmem, hbm],
         out_specs=vmem,
         scratch_shapes=[
+            pltpu.VMEM((T, width), BF16),
+            pltpu.VMEM(w_state.shape[1:], BF16),
             pltpu.VMEM((C, T), jnp.int32),
             pltpu.VMEM((2, width // 4, 2, chans), BF16),
             pltpu.VMEM((2, width, chans), BF16),
@@ -661,6 +672,7 @@
             pltpu.VMEM((HEAD_DIM, chans), F32),
             pltpu.VMEM((8, chans), F32),
             pltpu.VMEM((2, T, chans), BF16),
+            dma((2,)),
             dma((2,)),
             dma,
             dma((2,)),

time: 180 us -> 180 us (level)
  no operation moved by 1% of the time
where the time goes in v6:
time: 180 us
  Pallas kernels  178 us (99%)
  local copies, waits for them, and re-layouts  1.88 us (1%)
    pallas_call x1, Pallas kernels, per_device(): pl.pallas_call(functools.partial(layer_kernel, E, C), out_shape=jax.Shape...  178 us

profile of v6, /device:TPU:7, one launch (start us, length us, event | category | flops | bytes accessed | tf_op | source)
XLA Modules:
  0.0 179.6 jit_solution(2551595662529489408)
XLA Ops:
  0.0 177.7 %layer.1 = bf16[128,2048]{1,0:T(8,128)(2,1)} custom-call(s32[8,128]{1,0:T(8,128)} %bitcast.19, bf16[128,2048]{1,0:T(8,128)(2,1)} %bitcast.16, bf16[2048,2,512]{2,1,0:T(2,128)(2,1)} %bitcast.13, bf16[2048,128]{1,0:T(8,128)(2,1)} %bitcast.17, bf16[8,2048]{1,0:T(8,128)(2,1)} %bitcast.18, f32[1,8]{1,0:T(1,128)} %bitcast.21, f32[1,8]{1,0:T(1,128)} %bitcast.22, ...), custom_call_target="tpu_custom_call" | custom-call | tf_op jit(solution)/shard_map/layer/pallas_call | solution.py:645
  177.7 1.9 %copy.13 = bf16[1,128,2048]{2,1,0:T(8,128)(2,1)} copy(bf16[1,128,2048]{2,1,0:T(8,128)(2,1)} %bitcast.15) | data formatting | bytes 1048576
